TPU v7x, 256 devices: a whole 4x4x8 slice. The times are simulated.
256 devices in a mesh: blk: 8 (over y, x_hi), dom: 32 (over z, x_lo, core).
Axes of the slice: x: 4 (x_hi: 2, x_lo: 2; x = x_hi * 2 + x_lo), y: 4, z: 8, core: 2. Of those that a mesh axis runs over, the one named last changes fastest.
Arguments:
- cell_features: bfloat16 [32, 2048, 768], P('dom', 'blk'), may hold values from -6 to 6
- cotangent: bfloat16 [32, 2048, 768], P('dom', 'blk'), may hold values from -6 to 6
- query_weight: bfloat16 [768, 768], replicated
- key_weight: bfloat16 [768, 768], replicated
- value_weight: bfloat16 [768, 768], replicated, may hold values from -0.21875 to 0.21875
- out_weight: bfloat16 [768, 768], replicated, may hold values from -0.21875 to 0.21875
- anchor_index: int32 [32, 256], P('dom', 'blk'), may hold values from 0 to 255, as said below
- face_cells: int32 [32, 8, 2, 128], P('dom', 'blk'), may hold values from 0 to 255, as said below
- halo_count: int32 [32, 8, 2], P('dom', 'blk'), may hold values from 0 to 128, as said below
- neighbour_blocks: int32 [32, 16, 3], P('dom', 'blk'), may hold values from 0 to 3, as said below
Outputs:
- mixed: bfloat16 [32, 2048, 768], P('dom', 'blk')
- cell_grad: bfloat16 [32, 2048, 768], P('dom', 'blk')
- weight_grads: float32 [3072, 768], P(('blk', 'dom'))
Inputs may be any that keep to these rules, and one draw needn't show every extreme that they name: `anchor_index`: the 32 entries of one slot are different cells of that slot. `face_cells`: the 256 entries of one slot are different cells of that slot. halo_count[0, b, 0] and halo_count[31, b, 1] are 0 for every b; all other entries are 1 or more. `neighbour_blocks`: row b*2+j lists 3 different pool blocks, the first of them j itself.
All inputs are finite; a program needn't handle non-finite values.
Results may differ from a plain program's by a relative error of at most 0.017.
The roundings to bfloat16 on the way count: a program that leaves them out, or rounds other values in their place, can miss the bound.
Values may be sent and summed in bfloat16 or wider, within the bound.
No kernel may reach another device: no remote copies, remote signals or barrier semaphores. Data moves between devices by JAX's collectives and lax.ppermute only.
A program may use at most 128 MiB of HBM per device.

v0:
```python
import functools

import jax
import jax.numpy as jnp
from jax import lax
from jax.experimental import pallas as pl
from jax.experimental.pallas import tpu as pltpu
from jax.sharding import Mesh, PartitionSpec as P

HEADS = 12
BS = 128
NB = 3
D = 768
CELLS = 256
ANCHORS = 256
POOL_ROWS = 512
KEY_ROWS = 768
HEAD = 64
SIDE = 384
PAIRS = 3
OTHERS = 7
PAIR = 128
SCALE = 0.125
EPSILON = 1e-06
MASKED = -1e30

f32 = jnp.float32
bf16 = jnp.bfloat16

NN = (((1,), (0,)), ((), ()))
NT = (((1,), (1,)), ((), ()))
TN = (((0,), (0,)), ((), ()))


def dot(a, b, dims=NN):
    return lax.dot_general(a, b, dims, preferred_element_type=f32)


def params(mib):
    return pltpu.CompilerParams(vmem_limit_bytes=mib << 20)


def send_kernel(x_ref, anchor_ref, face_ref, normed_ref, rows_a_ref, rows_lo_ref, rows_hi_ref):
    x = x_ref[...].astype(f32)
    inverse = lax.rsqrt(jnp.mean(x * x, axis=-1, keepdims=True) + EPSILON)
    normed = (x * inverse).astype(bf16)
    normed_ref[...] = normed

    def picked(index_row):
        cells = lax.broadcasted_iota(jnp.int32, (CELLS, index_row.shape[1]), 0)
        one_hot = (cells == index_row).astype(bf16)
        return dot(one_hot, normed, TN).astype(bf16)

    rows_a_ref[...] = picked(anchor_ref[...])
    rows_lo_ref[...] = picked(face_ref[0:1, :])
    rows_hi_ref[...] = picked(face_ref[1:2, :])


def send_call(x, anchor_row, face_rows):
    shapes = [(CELLS, D), (32, D), (BS, D), (BS, D)]
    return pl.pallas_call(
        send_kernel,
        out_shape=[jax.ShapeDtypeStruct(s, bf16) for s in shapes],
        compiler_params=params(8),
    )(x, anchor_row, face_rows)


def project_kernel(n_ref, dy_ref, wq_ref, wk_ref, wv_ref, wo_ref, q_ref, k_ref, v_ref, g_ref):
    normed = n_ref[...]
    q_ref[...] = (dot(normed, wq_ref[...]).astype(bf16) * SCALE).astype(bf16)
    k_ref[...] = dot(normed, wk_ref[...]).astype(bf16)
    v_ref[...] = dot(normed, wv_ref[...]).astype(bf16)
    g_ref[...] = dot(dy_ref[...], wo_ref[...], NT).astype(bf16)


def project_call(normed, dy, wq, wk, wv, wo):
    return pl.pallas_call(
        project_kernel,
        out_shape=[jax.ShapeDtypeStruct((CELLS, D), bf16)] * 4,
        compiler_params=params(14),
    )(normed, dy, wq, wk, wv, wo)


def attend_kernel(extra, near_ref, count_ref, side_ref, q_ref, k_ref, v_ref, g_ref, n_ref, lo_ref,
                  hi_ref, dy_ref, wk_ref, wv_ref, *refs):
    anchor_refs = refs[:OTHERS + 1]
    out_ref, keys, values, keys_t, values_t, bias, outside = refs[OTHERS + 1:]
    outside[0:BS, :] = lo_ref[...]
    outside[BS:2 * BS, :] = hi_ref[...]
    for index, rows in enumerate(anchor_refs):
        outside[2 * BS + 32 * index:2 * BS + 32 * index + 32, :] = rows[...]
    if extra:
        out_ref[1024:1024 + KEY_ROWS, :CELLS] = n_ref[...].T
        out_ref[1024:1024 + KEY_ROWS, CELLS:] = outside[...].T
        out_ref[1024 + KEY_ROWS:, :] = dy_ref[...]
    first = pl.multiple_of(side_ref[0] * SIDE, SIDE)
    mine = pl.ds(first, SIDE)
    keys[0:CELLS, :] = k_ref[:, mine]
    values[0:CELLS, :] = v_ref[:, mine]
    keys[CELLS:, :] = dot(outside[...], wk_ref[:, mine]).astype(bf16)
    values[CELLS:, :] = dot(outside[...], wv_ref[:, mine]).astype(bf16)
    keys_t[...] = keys[...].T
    values_t[...] = values[...].T

    row = lax.broadcasted_iota(jnp.int32, (BS, BS), 0)
    for block in range(4):
        for j in range(2):
            used = (near_ref[j, 0] == block) | (near_ref[j, 1] == block) | (near_ref[j, 2] == block)
            live = jnp.where(used, BS if block < 2 else count_ref[max(block - 2, 0)], 0)
            bias[block * BS:(block + 1) * BS, j * BS:(j + 1) * BS] = jnp.where(row < live, 0.0, MASKED)

    lane = lax.broadcasted_iota(jnp.int32, (CELLS, PAIR), 1)

    def softmax(scores):
        highest = jnp.max(scores, axis=0, keepdims=True)
        powers = jnp.exp(scores - highest)
        return powers * (1.0 / jnp.sum(powers, axis=0, keepdims=True))

    def score_grad(probs, prob_grad):
        weighted = probs * prob_grad
        return weighted - probs * jnp.sum(weighted, axis=0, keepdims=True)

    for pair in range(PAIRS):
        cols = slice(pair * PAIR, (pair + 1) * PAIR)
        k_pair = keys[:, cols]
        v_pair = values[:, cols]
        from_cols = pl.ds(pl.multiple_of(first + pair * PAIR, PAIR), PAIR)
        q_pair = q_ref[:, from_cols]
        g_pair = g_ref[:, from_cols]
        key_term = None
        value_term = None
        out_t = []
        qg_t = []
        for half in range(2):
            chosen = (lane >= HEAD) if half else (lane < HEAD)
            q_head = jnp.where(chosen, q_pair, jnp.zeros_like(q_pair))
            g_head = jnp.where(chosen, g_pair, jnp.zeros_like(g_pair))
            scores = dot(k_pair, q_head, NT)
            prob_grad = dot(v_pair, g_head, NT)
            near = softmax(scores[:POOL_ROWS] + bias[...])
            anchor = softmax(scores[POOL_ROWS:])
            probs = jnp.concatenate([near.astype(bf16), anchor.astype(bf16)], 0)
            grads = jnp.concatenate(
                [
                    score_grad(near, prob_grad[:POOL_ROWS]).astype(bf16),
                    score_grad(anchor, prob_grad[POOL_ROWS:]).astype(bf16),
                ],
                0,
            )
            head_rows = slice(pair * PAIR + half * HEAD, pair * PAIR + (half + 1) * HEAD)
            out_t.append(dot(values_t[head_rows, :], probs))
            qg_t.append(dot(keys_t[head_rows, :], grads) * SCALE)
            k_new = dot(grads, q_head)
            v_new = dot(probs, g_head)
            key_term = k_new if key_term is None else key_term + k_new
            value_term = v_new if value_term is None else value_term + v_new
        shifted_cols = slice(SIDE + pair * PAIR, SIDE + (pair + 1) * PAIR)
        out_ref[CELLS:CELLS + KEY_ROWS, cols] = key_term.astype(bf16)
        out_ref[CELLS:CELLS + KEY_ROWS, shifted_cols] = value_term.astype(bf16)
        out_ref[0:CELLS, cols] = jnp.concatenate(out_t, 0).astype(bf16).T
        out_ref[0:CELLS, shifted_cols] = jnp.concatenate(qg_t, 0).astype(bf16).T


def attend_call(extra, near, count, side, q, k, v, g, normed, lo, hi, dy, wk, wv, anchors):
    smem = pl.BlockSpec(memory_space=pltpu.SMEM)
    vmem = pl.BlockSpec(memory_space=pltpu.VMEM)
    return pl.pallas_call(
        functools.partial(attend_kernel, extra),
        in_specs=[smem] * 3 + [vmem] * (11 + OTHERS),
        out_shape=jax.ShapeDtypeStruct((2048 if extra else 1024, D), bf16),
        scratch_shapes=[
            pltpu.VMEM((KEY_ROWS, SIDE), bf16),
            pltpu.VMEM((KEY_ROWS, SIDE), bf16),
            pltpu.VMEM((SIDE, KEY_ROWS), bf16),
            pltpu.VMEM((SIDE, KEY_ROWS), bf16),
            pltpu.VMEM((POOL_ROWS, CELLS), f32),
            pltpu.VMEM((POOL_ROWS, D), bf16),
        ],
        compiler_params=params(24),
    )(near, count, side, q, k, v, g, normed, lo, hi, dy, wk, wv, *anchors)


def outer_kernel(first_ref, own_ref, got_ref, parts):
    mine = slice(1024, 1024 + KEY_ROWS)

    def block(term, low, cols):
        rows = [term[m + 24 * low:m + 24 * low + 24, cols] for m in range(0, term.shape[0], 48)]
        return jnp.concatenate(rows, 0).astype(bf16)

    def keep(matrix, term, cols):
        for high in range(2):
            for low in range(2):
                parts[4 * matrix + 2 * high + low] = block(term[high * SIDE:(high + 1) * SIDE], low, cols)

    left, right = slice(0, SIDE), slice(SIDE, D)
    keep(0, dot(first_ref[mine, :CELLS], own_ref[0:CELLS, right])
         + dot(got_ref[mine, :CELLS], got_ref[0:CELLS, right]), slice(None))
    pairs = (
        dot(first_ref[mine, :], own_ref[CELLS:1024, :])
        + dot(got_ref[mine, :], got_ref[CELLS:1024, :])
    )
    keep(1, pairs, left)
    keep(2, pairs, right)
    out_term = dot(own_ref[0:CELLS, left], first_ref[1024 + KEY_ROWS:, :], TN) + dot(
        got_ref[0:CELLS, left], got_ref[1024 + KEY_ROWS:, :], TN
    )
    for high in range(2):
        for low in range(2):
            parts[12 + 2 * high + low] = block(out_term, low, right if high else left)

def outer_call(first, own, got):
    return pl.pallas_call(
        outer_kernel,
        out_shape=jax.ShapeDtypeStruct((16, 192, SIDE), bf16),
        compiler_params=params(24),
    )(first, own, got)


def plane_kernel(got_ref, out_ref):
    total = got_ref[0].astype(f32)
    for index in range(1, 16):
        total = total + got_ref[index].astype(f32)
    for z in range(8):
        out_ref[z] = total[24 * z:24 * z + 24].astype(bf16)


def plane_call(got):
    return pl.pallas_call(
        plane_kernel,
        out_shape=jax.ShapeDtypeStruct((8, 24, SIDE), bf16),
        compiler_params=params(10),
    )(got)


def back_kernel(core_ref, x_ref, first_ref, own_ref, wq_ref, wk_ref, wv_ref, wo_ref,
                mixed_ref, ng_ref, lo_ref, hi_ref, *anchor_refs):
    core = core_ref[0]
    kv = None
    extra = None
    out = x_ref[...].astype(f32)
    for source, side in ((own_ref, core), (first_ref, 1 - core)):
        half = pl.ds(pl.multiple_of(side * SIDE, SIDE), SIDE)
        term = dot(source[CELLS:1024, :SIDE], wk_ref[:, half], NT)
        kv = term if kv is None else kv + term
        kv = kv + dot(source[CELLS:1024, SIDE:], wv_ref[:, half], NT)
        term = dot(source[0:CELLS, SIDE:], wq_ref[:, half], NT)
        extra = term if extra is None else extra + term
        out = out + dot(source[0:CELLS, :SIDE], wo_ref[half, :])
    ng_ref[...] = kv[:CELLS] + extra
    lo_ref[...] = kv[CELLS:CELLS + BS].astype(bf16)
    hi_ref[...] = kv[CELLS + BS:POOL_ROWS].astype(bf16)
    for index, rows in enumerate(anchor_refs):
        rows[...] = kv[POOL_ROWS + 32 * index:POOL_ROWS + 32 * index + 32].astype(bf16)
    mixed_ref[...] = out.astype(bf16)


def back_call(core, x, first, own, wq, wk, wv, wo):
    smem = pl.BlockSpec(memory_space=pltpu.SMEM)
    vmem = pl.BlockSpec(memory_space=pltpu.VMEM)
    return pl.pallas_call(
        back_kernel,
        in_specs=[smem] + [vmem] * 7,
        out_shape=[
            jax.ShapeDtypeStruct((CELLS, D), bf16),
            jax.ShapeDtypeStruct((CELLS, D), f32),
            jax.ShapeDtypeStruct((BS, D), bf16),
            jax.ShapeDtypeStruct((BS, D), bf16),
        ] + [jax.ShapeDtypeStruct((32, D), bf16)] * (OTHERS + 1),
        compiler_params=params(24),
    )(core, x, first, own, wq, wk, wv, wo)


def final_kernel(x_ref, dy_ref, own_ref, lo_ref, hi_ref, anchor_ref, face_ref, *refs):
    rows_refs, out_ref = refs[:-1], refs[-1]
    x = x_ref[...].astype(f32)
    inverse = lax.rsqrt(jnp.mean(x * x, axis=-1, keepdims=True) + EPSILON)

    def placed(index_row, rows):
        cells = lax.broadcasted_iota(jnp.int32, (CELLS, index_row.shape[1]), 0)
        return dot((cells == index_row).astype(bf16), rows)

    shares = sum(rows[...].astype(f32) for rows in rows_refs)
    high = shares.astype(bf16)
    low = (shares - high.astype(f32)).astype(bf16)
    normed_grad = (
        own_ref[...]
        + placed(face_ref[0:1, :], lo_ref[...])
        + placed(face_ref[1:2, :], hi_ref[...])
        + placed(anchor_ref[...], high)
        + placed(anchor_ref[...], low)
    )
    cube = inverse * inverse * inverse
    out_ref[...] = (
        dy_ref[...].astype(f32)
        + inverse * normed_grad
        - x * cube * jnp.mean(normed_grad * x, axis=-1, keepdims=True)
    ).astype(bf16)


def final_call(x, dy, own, from_lo, from_hi, anchor_row, face_rows, shares):
    return pl.pallas_call(
        final_kernel,
        out_shape=jax.ShapeDtypeStruct((CELLS, D), bf16),
        compiler_params=params(12),
    )(x, dy, own, from_lo, from_hi, anchor_row, face_rows, *shares)


def swapped(value, axis):
    return lax.ppermute(value, axis, [(0, 1), (1, 0)])


def along(value, step):
    count = 32
    pairs = [(i, i + step) for i in range(count) if 0 <= i + step < count]
    return lax.ppermute(value, ("z", "xl", "core"), pairs)


SLOT_STEPS = [(dy, dx) for dy in range(4) for dx in range(2) if (dy, dx) != (0, 0)]
PLANE = ("y", "xh", "xl")


def to_slot(value, dy, dx):
    pairs = [
        (2 * y + h, 2 * ((y + dy) % 4) + (h + dx) % 2) for y in range(4) for h in range(2)
    ]
    return lax.ppermute(value, ("y", "xh"), pairs)


def settled(rows):
    pieces = rows.reshape(2, 12, SIDE)
    y, xh, core = (lax.axis_index(a) for a in ("y", "xh", "core"))
    last = y == 3
    pick = jnp.where(last, xh, core)
    own = lax.dynamic_index_in_dim(pieces, pick, 0, keepdims=False)
    other = lax.dynamic_index_in_dim(pieces, 1 - pick, 0, keepdims=False)

    def device(y_at, xh_at, core_at):
        return (y_at * 2 + xh_at) * 2 + core_at

    turn, swap = [], []
    for h in range(2):
        for r in range(2):
            turn.append((device(3, h, r), device(3, r, h)))
            swap.append((device(3, h, r), device(3, r, 1 - h)))
            swap += [(device(m, h, r), device(m, h, 1 - r)) for m in range(3)]
    axes = ("y", "xh", "core")
    turned = lax.ppermute(own, axes, turn)
    here = jnp.where(last, turned, own)
    there = lax.ppermute(other, axes, swap)
    return jnp.where(
        core == 0, jnp.concatenate([here, there], 1), jnp.concatenate([there, here], 1)
    )


def body(
    cell_features,
    cotangent,
    query_weight,
    key_weight,
    value_weight,
    out_weight,
    anchor_index,
    face_cells,
    halo_count,
    neighbour_blocks,
):
    x = cell_features[0]
    dy = cotangent[0]
    face_rows = face_cells.reshape(2, BS)
    near = neighbour_blocks.reshape(2, NB)
    count = halo_count.reshape(2)
    weights = (query_weight, key_weight, value_weight, out_weight)
    core = lax.axis_index("core").astype(jnp.int32).reshape(1)

    normed, sent_anchors, sent_lo, sent_hi = send_call(x, anchor_index, face_rows)
    anchors = [sent_anchors] + [to_slot(sent_anchors, -dy, dx) for dy, dx in SLOT_STEPS]
    from_lo = along(sent_hi, 1)
    from_hi = along(sent_lo, -1)
    q, k, v, g = project_call(normed, dy, *weights)

    common = (q, k, v, g, normed, from_lo, from_hi, dy, key_weight, value_weight, anchors)
    first = attend_call(True, near, count, 1 - core, *common)
    got = swapped(first, "core")
    own = attend_call(False, near, count, core, *common)

    parts = outer_call(first, own, got)
    plane = lax.all_to_all(parts, PLANE, 0, 0, tiled=True)
    column = lax.all_to_all(plane_call(plane), "z", 0, 0, tiled=True)
    weight_grads = settled(jnp.sum(column.astype(f32), axis=0))

    mixed, own_grad, to_lo, to_hi, *shares = back_call(core, x, first, own, *weights)
    back_hi = along(to_lo, -1)
    back_lo = along(to_hi, 1)
    shares = [shares[0]] + [
        to_slot(share, dy, dx) for share, (dy, dx) in zip(shares[1:], SLOT_STEPS)
    ]
    cell_grad = final_call(x, dy, own_grad, back_lo, back_hi, anchor_index, face_rows, shares)
    return mixed[None], cell_grad[None], weight_grads


def solution(mesh):
    fine = Mesh(mesh.devices.reshape(4, 2, 8, 2, 2), ("y", "xh", "z", "xl", "core"))
    dom = ("z", "xl", "core")
    blk = ("y", "xh")
    return jax.shard_map(
        body,
        mesh=fine,
        in_specs=(
            P(dom, blk, None),
            P(dom, blk, None),
            P(),
            P(),
            P(),
            P(),
            P(dom, blk),
            P(dom, blk, None, None),
            P(dom, blk, None),
            P(dom, blk, None),
        ),
        out_specs=(P(dom, blk, None), P(dom, blk, None), P(blk + dom, None)),
        check_vma=False,
    )
```

profile of v0, /device:TPU:24, one launch (start us, length us, event | category | flops | bytes accessed | tf_op | source)
XLA Modules:
  0.0 161.2 jit_solution(11105426326516493551)
XLA Ops:
  3.5 1.8 %collective-permute-start = (bf16[128,768]{1,0:T(8,128)(2,1)S(1)}, bf16[128,768]{1,0:T(8,128)(2,1)S(1)}, u32[]{:S(2)}, u32[]{:S(2)}) collective-permute-start(bf16[128,768]{1,0:T(8,128)(2,1)S(1)} %get-tuple-element.28), channel_id=1, source_target_pairs={{0,1},{1,2},{2,3},{3,4},{4,5},{5,6},{6,7},{7,8},{8,9},{9,10},{10,1... | collective-permute-start | bytes 589832 | tf_op jit(solution)/shard_map/ppermute | solution.py:315
  6.5 3.1 %collective-permute-start.2 = (bf16[32,768]{1,0:T(8,128)(2,1)S(1)}, bf16[32,768]{1,0:T(8,128)(2,1)S(1)}, u32[]{:S(2)}, u32[]{:S(2)}) collective-permute-start(bf16[32,768]{1,0:T(8,128)(2,1)S(1)} %get-tuple-element.30.refs_0_), channel_id=1, source_target_pairs={{0,32},{32,0},{64,96},{96,64},{128,160},{160,128},{192,224},{224,1... | collective-permute-start | bytes 147464 | tf_op jit(solution)/shard_map/ppermute | solution.py:326
  10.8 2.0 %collective-permute-done.2.refs_1_ = bf16[32,768]{1,0:T(8,128)(2,1)S(1)} collective-permute-done((bf16[32,768]{1,0:T(8,128)(2,1)S(1)}, bf16[32,768]{1,0:T(8,128)(2,1)S(1)}, u32[]{:S(2)}, u32[]{:S(2)}) %collective-permute-start.2) | collective-permute-done | bytes 49184 | tf_op jit(solution)/shard_map/ppermute | solution.py:326
  13.3 1.5 collective-permute-start.5
  15.5 3.9 %collective-permute-start.6 = (bf16[32,768]{1,0:T(8,128)(2,1)S(1)}, bf16[32,768]{1,0:T(8,128)(2,1)S(1)}, u32[]{:S(2)}, u32[]{:S(2)}) collective-permute-start(bf16[32,768]{1,0:T(8,128)(2,1)S(1)} %get-tuple-element.30.refs_0_), channel_id=1, source_target_pairs={{0,160},{32,128},{64,224},{96,192},{128,32},{160,0},{192,96},{224,... | collective-permute-start | bytes 147464 | tf_op jit(solution)/shard_map/ppermute | solution.py:326
  29.4 1.4 shard_map.122
  40.2 6.8 %shard_map.123.first_ref = bf16[2048,768]{1,0:T(8,128)(2,1)S(1)} custom-call(s32[2,3]{1,0:T(2,128)S(1)} %bitcast.19, s32[2]{0:T(128)S(1)} %bitcast.23, s32[1]{0:T(128)S(6)} %sub.6.side_ref, bf16[256,768]{1,0:T(8,128)(2,1)S(1)} %get-tuple-element.24.q_ref, bf16[256,768]{1,0:T(8,128)(2,1)S(1)} %get-tuple-element.25.k_ref, ...), custom_call_target="tpu_custom_call" | custom-call | tf_op jit(solution)/shard_map/pallas_call | solution.py:167
  48.0 6.8 %shard_map.124.own_ref = bf16[1024,768]{1,0:T(8,128)(2,1)S(1)} custom-call(s32[2,3]{1,0:T(2,128)S(1)} %bitcast.20, s32[2]{0:T(128)S(1)} %bitcast.24, s32[1]{0:T(128)} %bitcast.side_ref.core_ref, bf16[256,768]{1,0:T(8,128)(2,1)S(1)} %get-tuple-element.24.q_ref, bf16[256,768]{1,0:T(8,128)(2,1)S(1)} %get-tuple-element.25.k_ref, ...), custom_call_target="tpu_custom_call" | custom-call | tf_op jit(solution)/shard_map/pallas_call | solution.py:167
  54.8 2.7 %shard_map.127 = bf16[16,192,384]{2,1,0:T(8,128)(2,1)S(1)} custom-call(bf16[2048,768]{1,0:T(8,128)(2,1)S(1)} %shard_map.123.first_ref, bf16[1024,768]{1,0:T(8,128)(2,1)S(1)} %shard_map.124.own_ref, bf16[2048,768]{1,0:T(8,128)(2,1)S(1)} %collective-permute-done.18.got_ref), custom_call_target="tpu_custom_call" | custom-call | tf_op jit(solution)/shard_map/pallas_call | solution.py:212
  57.5 38.3 %all_to_all.10.got_ref = bf16[16,192,384]{2,1,0:T(8,128)(2,1)S(1)} all-to-all(bf16[16,192,384]{2,1,0:T(8,128)(2,1)S(1)} %shard_map.127), channel_id=1, replica_groups=mesh['y'=4,'xh'=2,'z'=8,'xl'=2,'core'=2] {'y','xh','xl'}, dimensions={0} | all-to-all | bytes 4718592 | tf_op jit(solution)/shard_map/all_to_all | solution.py:387
  96.8 10.8 %all-to-all-start.1 = ((bf16[8,24,384]{2,1,0:T(8,128)(2,1)}), bf16[8,24,384]{2,1,0:T(8,128)(2,1)}, u32[]{:S(2)}, u32[]{:S(2)}) async-start(bf16[8,24,384]{2,1,0:T(8,128)(2,1)} %copy-done.27), calls=%async_computation.1 | async-start | bytes 294912 | tf_op jit(solution)/shard_map/all_to_all | solution.py:388
  110.2 1.4 copy-done.7
  115.1 4.2 %shard_map.125 = (bf16[256,768]{1,0:T(8,128)(2,1)}, f32[256,768]{1,0:T(8,128)S(1)}, bf16[128,768]{1,0:T(8,128)(2,1)S(1)}, bf16[128,768]{1,0:T(8,128)(2,1)S(1)}, ...) custom-call(s32[1]{0:T(128)} %bitcast.side_ref.core_ref, ...), custom_call_target="tpu_custom_call" | custom-call | tf_op jit(solution)/shard_map/pallas_call | solution.py:260
  128.4 3.0 %collective-permute-start.9 = (bf16[128,768]{1,0:T(8,128)(2,1)}, bf16[128,768]{1,0:T(8,128)(2,1)S(1)}, u32[]{:S(2)}, u32[]{:S(2)}) collective-permute-start(bf16[128,768]{1,0:T(8,128)(2,1)} %copy-done.53), channel_id=1, source_target_pairs={{0,1},{1,2},{2,3},{3,4},{4,5},{5,6},{6,7},{7,8},{8,9},{9,10},{10,1... | collective-permute-start | bytes 589832 | tf_op jit(solution)/shard_map/ppermute | solution.py:315
  131.5 2.4 %collective-permute-start.12 = (bf16[32,768]{1,0:T(8,128)(2,1)}, bf16[32,768]{1,0:T(8,128)(2,1)S(1)}, u32[]{:S(2)}, u32[]{:S(2)}) collective-permute-start(bf16[32,768]{1,0:T(8,128)(2,1)} %copy-done.60), channel_id=1, source_target_pairs={{0,64},{32,96},{64,128},{96,160},{128,192},{160,224},{192,0},{224,... | collective-permute-start | bytes 147464 | tf_op jit(solution)/shard_map/ppermute | solution.py:326
  133.9 2.1 %collective-permute-start.13 = (bf16[32,768]{1,0:T(8,128)(2,1)}, bf16[32,768]{1,0:T(8,128)(2,1)S(1)}, u32[]{:S(2)}, u32[]{:S(2)}) collective-permute-start(bf16[32,768]{1,0:T(8,128)(2,1)} %copy-done.59), channel_id=1, source_target_pairs={{0,96},{32,64},{64,160},{96,128},{128,224},{160,192},{192,32},{224... | collective-permute-start | bytes 147464 | tf_op jit(solution)/shard_map/ppermute | solution.py:326
  136.0 1.6 %collective-permute-start.14 = (bf16[32,768]{1,0:T(8,128)(2,1)}, bf16[32,768]{1,0:T(8,128)(2,1)S(1)}, u32[]{:S(2)}, u32[]{:S(2)}) collective-permute-start(bf16[32,768]{1,0:T(8,128)(2,1)} %copy-done.58), channel_id=1, source_target_pairs={{0,128},{32,160},{64,192},{96,224},{128,0},{160,32},{192,64},{224,... | collective-permute-start | bytes 147464 | tf_op jit(solution)/shard_map/ppermute | solution.py:326
  138.6 2.8 %collective-permute-start.15 = (bf16[32,768]{1,0:T(8,128)(2,1)}, bf16[32,768]{1,0:T(8,128)(2,1)S(1)}, u32[]{:S(2)}, u32[]{:S(2)}) collective-permute-start(bf16[32,768]{1,0:T(8,128)(2,1)} %copy-done.57), channel_id=1, source_target_pairs={{0,160},{32,128},{64,224},{96,192},{128,32},{160,0},{192,96},{224,... | collective-permute-start | bytes 147464 | tf_op jit(solution)/shard_map/ppermute | solution.py:326
  141.4 1.5 collective-permute-start.16
  142.9 2.1 %collective-permute-start.17 = (bf16[32,768]{1,0:T(8,128)(2,1)}, bf16[32,768]{1,0:T(8,128)(2,1)S(1)}, u32[]{:S(2)}, u32[]{:S(2)}) collective-permute-start(bf16[32,768]{1,0:T(8,128)(2,1)} %copy-done.55), channel_id=1, source_target_pairs={{0,224},{32,192},{64,32},{96,0},{128,96},{160,64},{192,160},{224,1... | collective-permute-start | bytes 147464 | tf_op jit(solution)/shard_map/ppermute | solution.py:326
  145.0 2.0 %collective-permute-done.15.refs_5_ = bf16[32,768]{1,0:T(8,128)(2,1)S(1)} collective-permute-done((bf16[32,768]{1,0:T(8,128)(2,1)}, bf16[32,768]{1,0:T(8,128)(2,1)S(1)}, u32[]{:S(2)}, u32[]{:S(2)}) %collective-permute-start.15) | collective-permute-done | bytes 49184 | tf_op jit(solution)/shard_map/ppermute | solution.py:326
  147.7 3.1 %collective-permute-done.17.refs_7_ = bf16[32,768]{1,0:T(8,128)(2,1)S(1)} collective-permute-done((bf16[32,768]{1,0:T(8,128)(2,1)}, bf16[32,768]{1,0:T(8,128)(2,1)S(1)}, u32[]{:S(2)}, u32[]{:S(2)}) %collective-permute-start.17) | collective-permute-done | bytes 49184 | tf_op jit(solution)/shard_map/ppermute | solution.py:326
  153.8 1.5 shard_map.126
  155.3 5.3 %collective-permute-done.20 = f32[12,384]{1,0:T(8,128)S(1)} collective-permute-done((f32[12,384]{1,0:T(8,128)S(1)}, f32[12,384]{1,0:T(8,128)S(1)}, u32[]{:S(2)}, u32[]{:S(2)}) %collective-permute-start.20) | collective-permute-done | bytes 18464 | tf_op jit(solution)/shard_map/ppermute | solution.py:349
  (156 shorter events, 48.0 us)
Async XLA Ops:
  3.5 29.3 %collective-permute-start = (bf16[128,768]{1,0:T(8,128)(2,1)S(1)}, bf16[128,768]{1,0:T(8,128)(2,1)S(1)}, u32[]{:S(2)}, u32[]{:S(2)}) collective-permute-start(bf16[128,768]{1,0:T(8,128)(2,1)S(1)} %get-tuple-element.28), channel_id=1, source_target_pairs={{0,1},{1,2},{2,3},{3,4},{4,5},{5,6},{6,7},{7,8},{8,9},{9,10},{10,1... | collective-permute-start | bytes 589832 | tf_op jit(solution)/shard_map/ppermute | solution.py:315
  5.2 28.2 %collective-permute-start.1 = (bf16[128,768]{1,0:T(8,128)(2,1)S(1)}, bf16[128,768]{1,0:T(8,128)(2,1)S(1)}, u32[]{:S(2)}, u32[]{:S(2)}) collective-permute-start(bf16[128,768]{1,0:T(8,128)(2,1)S(1)} %get-tuple-element.29), channel_id=1, source_target_pairs={{1,0},{2,1},{3,2},{4,3},{5,4},{6,5},{7,6},{8,7},{9,8},{10,9},{11,1... | collective-permute-start | bytes 589832 | tf_op jit(solution)/shard_map/ppermute | solution.py:315
  6.5 6.2 %collective-permute-start.2 = (bf16[32,768]{1,0:T(8,128)(2,1)S(1)}, bf16[32,768]{1,0:T(8,128)(2,1)S(1)}, u32[]{:S(2)}, u32[]{:S(2)}) collective-permute-start(bf16[32,768]{1,0:T(8,128)(2,1)S(1)} %get-tuple-element.30.refs_0_), channel_id=1, source_target_pairs={{0,32},{32,0},{64,96},{96,64},{128,160},{160,128},{192,224},{224,1... | collective-permute-start | bytes 147464 | tf_op jit(solution)/shard_map/ppermute | solution.py:326
  9.6 5.3 %collective-permute-start.3 = (bf16[32,768]{1,0:T(8,128)(2,1)S(1)}, bf16[32,768]{1,0:T(8,128)(2,1)S(1)}, u32[]{:S(2)}, u32[]{:S(2)}) collective-permute-start(bf16[32,768]{1,0:T(8,128)(2,1)S(1)} %get-tuple-element.30.refs_0_), channel_id=1, source_target_pairs={{0,192},{32,224},{64,0},{96,32},{128,64},{160,96},{192,128},{224,1... | collective-permute-start | bytes 147464 | tf_op jit(solution)/shard_map/ppermute | solution.py:326
  10.4 9.1 %collective-permute-start.4 = (bf16[32,768]{1,0:T(8,128)(2,1)S(1)}, bf16[32,768]{1,0:T(8,128)(2,1)S(1)}, u32[]{:S(2)}, u32[]{:S(2)}) collective-permute-start(bf16[32,768]{1,0:T(8,128)(2,1)S(1)} %get-tuple-element.30.refs_0_), channel_id=1, source_target_pairs={{0,224},{32,192},{64,32},{96,0},{128,96},{160,64},{192,160},{224,1... | collective-permute-start | bytes 147464 | tf_op jit(solution)/shard_map/ppermute | solution.py:326
  13.3 8.0 %collective-permute-start.5 = (bf16[32,768]{1,0:T(8,128)(2,1)S(1)}, bf16[32,768]{1,0:T(8,128)(2,1)S(1)}, u32[]{:S(2)}, u32[]{:S(2)}) collective-permute-start(bf16[32,768]{1,0:T(8,128)(2,1)S(1)} %get-tuple-element.30.refs_0_), channel_id=1, source_target_pairs={{0,128},{32,160},{64,192},{96,224},{128,0},{160,32},{192,64},{224,... | collective-permute-start | bytes 147464 | tf_op jit(solution)/shard_map/ppermute | solution.py:326
  15.5 15.3 %collective-permute-start.6 = (bf16[32,768]{1,0:T(8,128)(2,1)S(1)}, bf16[32,768]{1,0:T(8,128)(2,1)S(1)}, u32[]{:S(2)}, u32[]{:S(2)}) collective-permute-start(bf16[32,768]{1,0:T(8,128)(2,1)S(1)} %get-tuple-element.30.refs_0_), channel_id=1, source_target_pairs={{0,160},{32,128},{64,224},{96,192},{128,32},{160,0},{192,96},{224,... | collective-permute-start | bytes 147464 | tf_op jit(solution)/shard_map/ppermute | solution.py:326
  20.0 11.4 %collective-permute-start.7 = (bf16[32,768]{1,0:T(8,128)(2,1)S(1)}, bf16[32,768]{1,0:T(8,128)(2,1)S(1)}, u32[]{:S(2)}, u32[]{:S(2)}) collective-permute-start(bf16[32,768]{1,0:T(8,128)(2,1)S(1)} %get-tuple-element.30.refs_0_), channel_id=1, source_target_pairs={{0,64},{32,96},{64,128},{96,160},{128,192},{160,224},{192,0},{224,... | collective-permute-start | bytes 147464 | tf_op jit(solution)/shard_map/ppermute | solution.py:326
  22.0 10.1 %collective-permute-start.8 = (bf16[32,768]{1,0:T(8,128)(2,1)S(1)}, bf16[32,768]{1,0:T(8,128)(2,1)S(1)}, u32[]{:S(2)}, u32[]{:S(2)}) collective-permute-start(bf16[32,768]{1,0:T(8,128)(2,1)S(1)} %get-tuple-element.30.refs_0_), channel_id=1, source_target_pairs={{0,96},{32,64},{64,160},{96,128},{128,224},{160,192},{192,32},{224... | collective-permute-start | bytes 147464 | tf_op jit(solution)/shard_map/ppermute | solution.py:326
  47.0 7.7 %collective-permute-start.18 = (bf16[2048,768]{1,0:T(8,128)(2,1)S(1)}, bf16[2048,768]{1,0:T(8,128)(2,1)S(1)}, u32[]{:S(2)}, u32[]{:S(2)}) collective-permute-start(bf16[2048,768]{1,0:T(8,128)(2,1)S(1)} %shard_map.123.first_ref), channel_id=1, source_target_pairs={{0,1},{1,0},{2,3},{3,2},{4,5},{5,4},{6,7},{7,6},{8,9},{9,8},{10,11... | collective-permute-start | bytes 9437192 | tf_op jit(solution)/shard_map/ppermute | solution.py:309
  96.8 40.9 %all-to-all-start.1 = ((bf16[8,24,384]{2,1,0:T(8,128)(2,1)}), bf16[8,24,384]{2,1,0:T(8,128)(2,1)}, u32[]{:S(2)}, u32[]{:S(2)}) async-start(bf16[8,24,384]{2,1,0:T(8,128)(2,1)} %copy-done.27), calls=%async_computation.1 | async-start | bytes 294912 | tf_op jit(solution)/shard_map/all_to_all | solution.py:388
  115.1 35.7 %copy-start.49 = (s32[1,1,2,128]{3,2,1,0:T(2,128)S(1)}, s32[1,1,2,128]{3,2,1,0:T(2,128)}, u32[]{:S(2)}) copy-start(s32[1,1,2,128]{3,2,1,0:T(2,128)} %param.17) | copy-start | bytes 3076
  115.1 35.7 %copy-start.52 = (s32[1,32]{1,0:T(1,128)S(1)}, s32[1,32]{1,0:T(1,128)}, u32[]{:S(2)}) copy-start(s32[1,32]{1,0:T(1,128)} %anchor_ref.3) | copy-start | bytes 388
  125.9 10.1 %collective-permute-start.11 = (bf16[32,768]{1,0:T(8,128)(2,1)}, bf16[32,768]{1,0:T(8,128)(2,1)S(1)}, u32[]{:S(2)}, u32[]{:S(2)}) collective-permute-start(bf16[32,768]{1,0:T(8,128)(2,1)} %get-tuple-element.36), channel_id=1, source_target_pairs={{0,32},{32,0},{64,96},{96,64},{128,160},{160,128},{192,224},{224,1... | collective-permute-start | bytes 147464 | tf_op jit(solution)/shard_map/ppermute | solution.py:326
  127.1 23.7 %collective-permute-start.10 = (bf16[128,768]{1,0:T(8,128)(2,1)}, bf16[128,768]{1,0:T(8,128)(2,1)S(1)}, u32[]{:S(2)}, u32[]{:S(2)}) collective-permute-start(bf16[128,768]{1,0:T(8,128)(2,1)} %copy-done.54), channel_id=1, source_target_pairs={{1,0},{2,1},{3,2},{4,3},{5,4},{6,5},{7,6},{8,7},{9,8},{10,9},{11,1... | collective-permute-start | bytes 589832 | tf_op jit(solution)/shard_map/ppermute | solution.py:315
  128.4 22.4 %collective-permute-start.9 = (bf16[128,768]{1,0:T(8,128)(2,1)}, bf16[128,768]{1,0:T(8,128)(2,1)S(1)}, u32[]{:S(2)}, u32[]{:S(2)}) collective-permute-start(bf16[128,768]{1,0:T(8,128)(2,1)} %copy-done.53), channel_id=1, source_target_pairs={{0,1},{1,2},{2,3},{3,4},{4,5},{5,6},{6,7},{7,8},{8,9},{9,10},{10,1... | collective-permute-start | bytes 589832 | tf_op jit(solution)/shard_map/ppermute | solution.py:315
  131.5 7.1 %collective-permute-start.12 = (bf16[32,768]{1,0:T(8,128)(2,1)}, bf16[32,768]{1,0:T(8,128)(2,1)S(1)}, u32[]{:S(2)}, u32[]{:S(2)}) collective-permute-start(bf16[32,768]{1,0:T(8,128)(2,1)} %copy-done.60), channel_id=1, source_target_pairs={{0,64},{32,96},{64,128},{96,160},{128,192},{160,224},{192,0},{224,... | collective-permute-start | bytes 147464 | tf_op jit(solution)/shard_map/ppermute | solution.py:326
  133.9 7.6 %collective-permute-start.13 = (bf16[32,768]{1,0:T(8,128)(2,1)}, bf16[32,768]{1,0:T(8,128)(2,1)S(1)}, u32[]{:S(2)}, u32[]{:S(2)}) collective-permute-start(bf16[32,768]{1,0:T(8,128)(2,1)} %copy-done.59), channel_id=1, source_target_pairs={{0,96},{32,64},{64,160},{96,128},{128,224},{160,192},{192,32},{224... | collective-permute-start | bytes 147464 | tf_op jit(solution)/shard_map/ppermute | solution.py:326
  136.0 6.9 %collective-permute-start.14 = (bf16[32,768]{1,0:T(8,128)(2,1)}, bf16[32,768]{1,0:T(8,128)(2,1)S(1)}, u32[]{:S(2)}, u32[]{:S(2)}) collective-permute-start(bf16[32,768]{1,0:T(8,128)(2,1)} %copy-done.58), channel_id=1, source_target_pairs={{0,128},{32,160},{64,192},{96,224},{128,0},{160,32},{192,64},{224,... | collective-permute-start | bytes 147464 | tf_op jit(solution)/shard_map/ppermute | solution.py:326
  138.6 8.5 %collective-permute-start.15 = (bf16[32,768]{1,0:T(8,128)(2,1)}, bf16[32,768]{1,0:T(8,128)(2,1)S(1)}, u32[]{:S(2)}, u32[]{:S(2)}) collective-permute-start(bf16[32,768]{1,0:T(8,128)(2,1)} %copy-done.57), channel_id=1, source_target_pairs={{0,160},{32,128},{64,224},{96,192},{128,32},{160,0},{192,96},{224,... | collective-permute-start | bytes 147464 | tf_op jit(solution)/shard_map/ppermute | solution.py:326
  141.4 6.3 %collective-permute-start.16 = (bf16[32,768]{1,0:T(8,128)(2,1)}, bf16[32,768]{1,0:T(8,128)(2,1)S(1)}, u32[]{:S(2)}, u32[]{:S(2)}) collective-permute-start(bf16[32,768]{1,0:T(8,128)(2,1)} %copy-done.56), channel_id=1, source_target_pairs={{0,192},{32,224},{64,0},{96,32},{128,64},{160,96},{192,128},{224,1... | collective-permute-start | bytes 147464 | tf_op jit(solution)/shard_map/ppermute | solution.py:326
  142.9 7.9 %collective-permute-start.17 = (bf16[32,768]{1,0:T(8,128)(2,1)}, bf16[32,768]{1,0:T(8,128)(2,1)S(1)}, u32[]{:S(2)}, u32[]{:S(2)}) collective-permute-start(bf16[32,768]{1,0:T(8,128)(2,1)} %copy-done.55), channel_id=1, source_target_pairs={{0,224},{32,192},{64,32},{96,0},{128,96},{160,64},{192,160},{224,1... | collective-permute-start | bytes 147464 | tf_op jit(solution)/shard_map/ppermute | solution.py:326
  147.1 8.2 %collective-permute-start.19 = (f32[12,384]{1,0:T(8,128)S(1)}, f32[12,384]{1,0:T(8,128)S(1)}, u32[]{:S(2)}, u32[]{:S(2)}) collective-permute-start(f32[12,384]{1,0:T(8,128)S(1)} %get-tuple-element.43), channel_id=1, source_target_pairs={{192,192},{193,224},{224,193},{225,225},{194,194},{195,226},{226,1... | collective-permute-start | bytes 55304 | tf_op jit(solution)/shard_map/ppermute | solution.py:347
  155.3 5.3 %collective-permute-start.20 = (f32[12,384]{1,0:T(8,128)S(1)}, f32[12,384]{1,0:T(8,128)S(1)}, u32[]{:S(2)}, u32[]{:S(2)}) collective-permute-start(f32[12,384]{1,0:T(8,128)S(1)} %get-tuple-element.44), channel_id=1, source_target_pairs={{192,193},{0,1},{64,65},{128,129},{193,225},{1,0},{65,64},{129,128... | collective-permute-start | bytes 55304 | tf_op jit(solution)/shard_map/ppermute | solution.py:349
  (59 other events, 161.2 us)
where the time goes:
time: 163 us; the launch traced here: 161 us
  starting transfers between devices  45.9 us (28%)
  blocking collectives  38.3 us (23%)
  local copies, waits for them, and re-layouts  37.8 us (23%)
  Pallas kernels  24.2 us (15%)
  waiting for transfers between devices  12.5 us (8%)
    all_to_all x1, blocking collectives, body(): plane = lax.all_to_all(parts, PLANE, 0, 0, tiled=True)  38.3 us
    unnamed x122, local copies, waits for them, and re-layouts  37.8 us
    ppermute x14, starting transfers between devices, to_slot(): return lax.ppermute(value, ('y', 'xh'), pairs)  26.1 us
    pallas_call x2, Pallas kernels, attend_call(): pl.pallas_call(functools.partial(attend_kernel, extra), in_specs=[smem] *...  13.6 us
    all_to_all x1, starting transfers between devices, body(): column = lax.all_to_all(plane_call(plane), 'z', 0, 0, tiled=True)  10.8 us
    ppermute x4, starting transfers between devices, along(): return lax.ppermute(value, ('z', 'xl', 'core'), pairs)  7.36 us
    ppermute x14, waiting for transfers between devices, to_slot(): return lax.ppermute(value, ('y', 'xh'), pairs)  7.16 us
    ppermute x1, waiting for transfers between devices, settled(): there = lax.ppermute(other, axes, swap)  5.32 us
  transfers between devices with their start and end apart: 22, of which 4 were waited for; matrix products, arithmetic and copies ran while one was open for 1% of the time, Pallas kernels for 9%

commit v1 on v0

--- a/solution.py
+++ b/solution.py
@@ -18,7 +18,7 @@
 HEAD = 64
 SIDE = 384
 PAIRS = 3
-OTHERS = 7
+SLOTS = 8
 PAIR = 128
 SCALE = 0.125
 EPSILON = 1e-06
@@ -34,6 +34,10 @@
 
 def dot(a, b, dims=NN):
     return lax.dot_general(a, b, dims, preferred_element_type=f32)
+
+
+def held(*arrays):
+    return [pltpu.with_memory_space_constraint(a, pltpu.HBM) for a in arrays]
 
 
 def params(mib):
@@ -51,18 +55,24 @@
         one_hot = (cells == index_row).astype(bf16)
         return dot(one_hot, normed, TN).astype(bf16)
 
-    rows_a_ref[...] = picked(anchor_ref[...])
+    anchor_rows = picked(anchor_ref[...])
+    for slot in range(SLOTS):
+        rows_a_ref[slot] = anchor_rows
     rows_lo_ref[...] = picked(face_ref[0:1, :])
     rows_hi_ref[...] = picked(face_ref[1:2, :])
 
 
 def send_call(x, anchor_row, face_rows):
-    shapes = [(CELLS, D), (32, D), (BS, D), (BS, D)]
     return pl.pallas_call(
         send_kernel,
-        out_shape=[jax.ShapeDtypeStruct(s, bf16) for s in shapes],
+        out_shape=[
+            pltpu.HBM((CELLS, D), bf16),
+            pltpu.HBM((SLOTS, 32, D), bf16),
+            jax.ShapeDtypeStruct((BS, D), bf16),
+            jax.ShapeDtypeStruct((BS, D), bf16),
+        ],
         compiler_params=params(8),
-    )(x, anchor_row, face_rows)
+    )(*held(x, anchor_row, face_rows))
 
 
 def project_kernel(n_ref, dy_ref, wq_ref, wk_ref, wv_ref, wo_ref, q_ref, k_ref, v_ref, g_ref):
@@ -78,27 +88,44 @@
         project_kernel,
         out_shape=[jax.ShapeDtypeStruct((CELLS, D), bf16)] * 4,
         compiler_params=params(14),
-    )(normed, dy, wq, wk, wv, wo)
-
-
-def attend_kernel(extra, near_ref, count_ref, side_ref, q_ref, k_ref, v_ref, g_ref, n_ref, lo_ref,
-                  hi_ref, dy_ref, wk_ref, wv_ref, *refs):
-    anchor_refs = refs[:OTHERS + 1]
-    out_ref, keys, values, keys_t, values_t, bias, outside = refs[OTHERS + 1:]
+    )(*held(normed, dy, wq, wk, wv, wo))
+
+
+def attend_first_kernel(near_ref, count_ref, side_ref, q_ref, k_ref, v_ref, g_ref, n_ref, lo_ref,
+                        hi_ref, an_ref, dy_ref, wk_ref, wv_ref, out_ref, rest_ref, keys, values,
+                        keys_t, values_t, bias, outside):
     outside[0:BS, :] = lo_ref[...]
     outside[BS:2 * BS, :] = hi_ref[...]
-    for index, rows in enumerate(anchor_refs):
-        outside[2 * BS + 32 * index:2 * BS + 32 * index + 32, :] = rows[...]
-    if extra:
-        out_ref[1024:1024 + KEY_ROWS, :CELLS] = n_ref[...].T
-        out_ref[1024:1024 + KEY_ROWS, CELLS:] = outside[...].T
-        out_ref[1024 + KEY_ROWS:, :] = dy_ref[...]
-    first = pl.multiple_of(side_ref[0] * SIDE, SIDE)
-    mine = pl.ds(first, SIDE)
+    for slot in range(SLOTS):
+        outside[2 * BS + 32 * slot:2 * BS + 32 * slot + 32, :] = an_ref[slot]
+    out_ref[1024:1024 + KEY_ROWS, :CELLS] = n_ref[...].T
+    out_ref[1024:1024 + KEY_ROWS, CELLS:] = outside[...].T
+    out_ref[1024 + KEY_ROWS:, :] = dy_ref[...]
+    side = side_ref[0]
+    mine = pl.ds(pl.multiple_of(side * SIDE, SIDE), SIDE)
+    rest = pl.ds(pl.multiple_of((1 - side) * SIDE, SIDE), SIDE)
     keys[0:CELLS, :] = k_ref[:, mine]
     values[0:CELLS, :] = v_ref[:, mine]
     keys[CELLS:, :] = dot(outside[...], wk_ref[:, mine]).astype(bf16)
     values[CELLS:, :] = dot(outside[...], wv_ref[:, mine]).astype(bf16)
+    rest_ref[:, :SIDE] = dot(outside[...], wk_ref[:, rest]).astype(bf16)
+    rest_ref[:, SIDE:] = dot(outside[...], wv_ref[:, rest]).astype(bf16)
+    attend(near_ref, count_ref, side, q_ref, g_ref, out_ref, keys, values, keys_t, values_t, bias)
+
+
+def attend_second_kernel(near_ref, count_ref, side_ref, q_ref, k_ref, v_ref, g_ref, rest_ref,
+                         out_ref, keys, values, keys_t, values_t, bias):
+    side = side_ref[0]
+    mine = pl.ds(pl.multiple_of(side * SIDE, SIDE), SIDE)
+    keys[0:CELLS, :] = k_ref[:, mine]
+    values[0:CELLS, :] = v_ref[:, mine]
+    keys[CELLS:, :] = rest_ref[:, :SIDE]
+    values[CELLS:, :] = rest_ref[:, SIDE:]
+    attend(near_ref, count_ref, side, q_ref, g_ref, out_ref, keys, values, keys_t, values_t, bias)
+
+
+def attend(near_ref, count_ref, side, q_ref, g_ref, out_ref, keys, values, keys_t, values_t, bias):
+    first = pl.multiple_of(side * SIDE, SIDE)
     keys_t[...] = keys[...].T
     values_t[...] = values[...].T
 
@@ -161,23 +188,38 @@
         out_ref[0:CELLS, shifted_cols] = jnp.concatenate(qg_t, 0).astype(bf16).T
 
 
-def attend_call(extra, near, count, side, q, k, v, g, normed, lo, hi, dy, wk, wv, anchors):
+def attend_scratch(extra):
+    return [
+        pltpu.VMEM((KEY_ROWS, SIDE), bf16),
+        pltpu.VMEM((KEY_ROWS, SIDE), bf16),
+        pltpu.VMEM((SIDE, KEY_ROWS), bf16),
+        pltpu.VMEM((SIDE, KEY_ROWS), bf16),
+        pltpu.VMEM((POOL_ROWS, CELLS), f32),
+    ] + [pltpu.VMEM((POOL_ROWS, D), bf16)] * extra
+
+
+def attend_first_call(near, count, side, queries, received, dy, wk, wv):
     smem = pl.BlockSpec(memory_space=pltpu.SMEM)
     vmem = pl.BlockSpec(memory_space=pltpu.VMEM)
     return pl.pallas_call(
-        functools.partial(attend_kernel, extra),
-        in_specs=[smem] * 3 + [vmem] * (11 + OTHERS),
-        out_shape=jax.ShapeDtypeStruct((2048 if extra else 1024, D), bf16),
-        scratch_shapes=[
-            pltpu.VMEM((KEY_ROWS, SIDE), bf16),
-            pltpu.VMEM((KEY_ROWS, SIDE), bf16),
-            pltpu.VMEM((SIDE, KEY_ROWS), bf16),
-            pltpu.VMEM((SIDE, KEY_ROWS), bf16),
-            pltpu.VMEM((POOL_ROWS, CELLS), f32),
-            pltpu.VMEM((POOL_ROWS, D), bf16),
-        ],
+        attend_first_kernel,
+        in_specs=[smem] * 3 + [vmem] * 11,
+        out_shape=[jax.ShapeDtypeStruct((2048, D), bf16), pltpu.HBM((POOL_ROWS, D), bf16)],
+        scratch_shapes=attend_scratch(1),
         compiler_params=params(24),
-    )(near, count, side, q, k, v, g, normed, lo, hi, dy, wk, wv, *anchors)
+    )(near, count, side, *queries[:4], *held(queries[4]), *received, *held(dy, wk, wv))
+
+
+def attend_second_call(near, count, side, queries, rest):
+    smem = pl.BlockSpec(memory_space=pltpu.SMEM)
+    vmem = pl.BlockSpec(memory_space=pltpu.VMEM)
+    return pl.pallas_call(
+        attend_second_kernel,
+        in_specs=[smem] * 3 + [vmem] * 5,
+        out_shape=jax.ShapeDtypeStruct((1024, D), bf16),
+        scratch_shapes=attend_scratch(0),
+        compiler_params=params(24),
+    )(near, count, side, *queries, *held(rest))
 
 
 def outer_kernel(first_ref, own_ref, got_ref, parts):
@@ -208,20 +250,19 @@
         for low in range(2):
             parts[12 + 2 * high + low] = block(out_term, low, right if high else left)
 
+
 def outer_call(first, own, got):
     return pl.pallas_call(
         outer_kernel,
-        out_shape=jax.ShapeDtypeStruct((16, 192, SIDE), bf16),
-        compiler_params=params(24),
+        out_shape=pltpu.HBM((16, 192, SIDE), bf16),
+        compiler_params=params(32),
     )(first, own, got)
 
 
 def plane_kernel(got_ref, out_ref):
-    total = got_ref[0].astype(f32)
-    for index in range(1, 16):
-        total = total + got_ref[index].astype(f32)
+    result = total([got_ref[index] for index in range(16)])
     for z in range(8):
-        out_ref[z] = total[24 * z:24 * z + 24].astype(bf16)
+        out_ref[z] = result[24 * z:24 * z + 24].astype(bf16)
 
 
 def plane_call(got):
@@ -232,9 +273,16 @@
     )(got)
 
 
-def back_kernel(core_ref, x_ref, first_ref, own_ref, wq_ref, wk_ref, wv_ref, wo_ref,
-                mixed_ref, ng_ref, lo_ref, hi_ref, *anchor_refs):
-    core = core_ref[0]
+def total(rows):
+    result = rows[0].astype(f32)
+    for row in rows[1:]:
+        result = result + row.astype(f32)
+    return result
+
+
+def back_kernel(place_ref, x_ref, first_ref, own_ref, wq_ref, wk_ref, wv_ref, wo_ref,
+                mixed_ref, ng_ref, lo_ref, hi_ref, a0_ref, a1_ref, a2_ref, a3_ref, rows):
+    core = place_ref[2]
     kv = None
     extra = None
     out = x_ref[...].astype(f32)
@@ -249,12 +297,14 @@
     ng_ref[...] = kv[:CELLS] + extra
     lo_ref[...] = kv[CELLS:CELLS + BS].astype(bf16)
     hi_ref[...] = kv[CELLS + BS:POOL_ROWS].astype(bf16)
-    for index, rows in enumerate(anchor_refs):
-        rows[...] = kv[POOL_ROWS + 32 * index:POOL_ROWS + 32 * index + 32].astype(bf16)
+    for y in range(4):
+        rows[y] = kv[POOL_ROWS + 64 * y:POOL_ROWS + 64 * y + 64].astype(bf16)
+    for step, target in enumerate((a0_ref, a1_ref, a2_ref, a3_ref)):
+        target[...] = rows[(place_ref[1] + step) % 4]
     mixed_ref[...] = out.astype(bf16)
 
 
-def back_call(core, x, first, own, wq, wk, wv, wo):
+def back_call(place, x, first, own, wq, wk, wv, wo):
     smem = pl.BlockSpec(memory_space=pltpu.SMEM)
     vmem = pl.BlockSpec(memory_space=pltpu.VMEM)
     return pl.pallas_call(
@@ -262,16 +312,38 @@
         in_specs=[smem] + [vmem] * 7,
         out_shape=[
             jax.ShapeDtypeStruct((CELLS, D), bf16),
-            jax.ShapeDtypeStruct((CELLS, D), f32),
+            pltpu.HBM((CELLS, D), f32),
             jax.ShapeDtypeStruct((BS, D), bf16),
             jax.ShapeDtypeStruct((BS, D), bf16),
-        ] + [jax.ShapeDtypeStruct((32, D), bf16)] * (OTHERS + 1),
+        ] + [jax.ShapeDtypeStruct((64, D), bf16)] * 4,
+        scratch_shapes=[pltpu.VMEM((4, 64, D), bf16)],
         compiler_params=params(24),
-    )(core, x, first, own, wq, wk, wv, wo)
-
-
-def final_kernel(x_ref, dy_ref, own_ref, lo_ref, hi_ref, anchor_ref, face_ref, *refs):
-    rows_refs, out_ref = refs[:-1], refs[-1]
+    )(place, *held(x, first, own, wq, wk, wv, wo))
+
+
+def share_kernel(place_ref, s0, s1, s2, s3, keep_ref, send_ref, rows):
+    summed = total([ref[...] for ref in (s0, s1, s2, s3)])
+    rows[0] = summed[:32]
+    rows[1] = summed[32:]
+    xh = place_ref[0] // 2
+    keep_ref[...] = rows[xh]
+    send_ref[...] = rows[1 - xh].astype(bf16)
+
+
+def share_call(place, shares):
+    smem = pl.BlockSpec(memory_space=pltpu.SMEM)
+    vmem = pl.BlockSpec(memory_space=pltpu.VMEM)
+    return pl.pallas_call(
+        share_kernel,
+        in_specs=[smem] + [vmem] * 4,
+        out_shape=[pltpu.HBM((32, D), f32), jax.ShapeDtypeStruct((32, D), bf16)],
+        scratch_shapes=[pltpu.VMEM((2, 32, D), f32)],
+        compiler_params=params(4),
+    )(place, *shares)
+
+
+def final_kernel(x_ref, dy_ref, own_ref, lo_ref, hi_ref, anchor_ref, face_ref, kept_ref, crossed_ref,
+                 out_ref):
     x = x_ref[...].astype(f32)
     inverse = lax.rsqrt(jnp.mean(x * x, axis=-1, keepdims=True) + EPSILON)
 
@@ -279,7 +351,7 @@
         cells = lax.broadcasted_iota(jnp.int32, (CELLS, index_row.shape[1]), 0)
         return dot((cells == index_row).astype(bf16), rows)
 
-    shares = sum(rows[...].astype(f32) for rows in rows_refs)
+    shares = kept_ref[...] + crossed_ref[...].astype(f32)
     high = shares.astype(bf16)
     low = (shares - high.astype(f32)).astype(bf16)
     normed_grad = (
@@ -297,16 +369,22 @@
     ).astype(bf16)
 
 
-def final_call(x, dy, own, from_lo, from_hi, anchor_row, face_rows, shares):
+def final_call(x, dy, own, from_lo, from_hi, anchor_row, face_rows, kept, crossed):
     return pl.pallas_call(
         final_kernel,
         out_shape=jax.ShapeDtypeStruct((CELLS, D), bf16),
         compiler_params=params(12),
-    )(x, dy, own, from_lo, from_hi, anchor_row, face_rows, *shares)
+    )(*held(x, dy, own), from_lo, from_hi, *held(anchor_row, face_rows, kept), crossed)
 
 
 def swapped(value, axis):
     return lax.ppermute(value, axis, [(0, 1), (1, 0)])
+
+
+def spread(arrays, axis):
+    return [arrays[0]] + [
+        lax.ppermute(arrays[k], axis, [(i, (i + k) % 4) for i in range(4)]) for k in (1, 2, 3)
+    ]
 
 
 def along(value, step):
@@ -315,24 +393,32 @@
     return lax.ppermute(value, ("z", "xl", "core"), pairs)
 
 
-SLOT_STEPS = [(dy, dx) for dy in range(4) for dx in range(2) if (dy, dx) != (0, 0)]
-PLANE = ("y", "xh", "xl")
-
-
-def to_slot(value, dy, dx):
-    pairs = [
-        (2 * y + h, 2 * ((y + dy) % 4) + (h + dx) % 2) for y in range(4) for h in range(2)
-    ]
-    return lax.ppermute(value, ("y", "xh"), pairs)
-
-
-def settled(rows):
-    pieces = rows.reshape(2, 12, SIDE)
-    y, xh, core = (lax.axis_index(a) for a in ("y", "xh", "core"))
-    last = y == 3
-    pick = jnp.where(last, xh, core)
-    own = lax.dynamic_index_in_dim(pieces, pick, 0, keepdims=False)
-    other = lax.dynamic_index_in_dim(pieces, 1 - pick, 0, keepdims=False)
+X_RING = ("xh", "xl")
+SLOT = ("y", "xh")
+
+
+def settle_kernel(place_ref, rows_ref, own_ref, other_ref):
+    rows = total([rows_ref[index] for index in range(8)])
+    upper = jnp.where(place_ref[1] == 3, place_ref[0] // 2, place_ref[2]) == 1
+    own_ref[...] = jnp.where(upper, rows[12:], rows[:12])
+    other_ref[...] = jnp.where(upper, rows[:12], rows[12:])
+
+
+def settle_call(place, rows):
+    smem = pl.BlockSpec(memory_space=pltpu.SMEM)
+    vmem = pl.BlockSpec(memory_space=pltpu.VMEM)
+    return pl.pallas_call(
+        settle_kernel,
+        in_specs=[smem, vmem],
+        out_shape=[jax.ShapeDtypeStruct((12, SIDE), f32)] * 2,
+        compiler_params=params(4),
+    )(place, rows)
+
+
+def settled(place, rows):
+    own, other = settle_call(place, rows)
+    last = place[1] == 3
+    core = place[2]
 
     def device(y_at, xh_at, core_at):
         return (y_at * 2 + xh_at) * 2 + core_at
@@ -371,30 +457,41 @@
     count = halo_count.reshape(2)
     weights = (query_weight, key_weight, value_weight, out_weight)
     core = lax.axis_index("core").astype(jnp.int32).reshape(1)
+    place = jnp.stack(
+        [2 * lax.axis_index("xh") + lax.axis_index("xl"), lax.axis_index("y"), core[0]]
+    ).astype(jnp.int32)
 
     normed, sent_anchors, sent_lo, sent_hi = send_call(x, anchor_index, face_rows)
-    anchors = [sent_anchors] + [to_slot(sent_anchors, -dy, dx) for dy, dx in SLOT_STEPS]
     from_lo = along(sent_hi, 1)
     from_hi = along(sent_lo, -1)
+    anchors = lax.all_to_all(sent_anchors, SLOT, 0, 0, tiled=True)
     q, k, v, g = project_call(normed, dy, *weights)
 
-    common = (q, k, v, g, normed, from_lo, from_hi, dy, key_weight, value_weight, anchors)
-    first = attend_call(True, near, count, 1 - core, *common)
+    first, rest = attend_first_call(
+        near, count, 1 - core, (q, k, v, g, normed), (from_lo, from_hi, anchors), dy,
+        key_weight, value_weight,
+    )
     got = swapped(first, "core")
-    own = attend_call(False, near, count, core, *common)
+    own = attend_second_call(near, count, core, (q, k, v, g), rest)
 
     parts = outer_call(first, own, got)
-    plane = lax.all_to_all(parts, PLANE, 0, 0, tiled=True)
-    column = lax.all_to_all(plane_call(plane), "z", 0, 0, tiled=True)
-    weight_grads = settled(jnp.sum(column.astype(f32), axis=0))
-
-    mixed, own_grad, to_lo, to_hi, *shares = back_call(core, x, first, own, *weights)
+    own, parts = lax.optimization_barrier((own, parts))
+    plane = lax.all_to_all(parts, ("y", "xh", "xl"), 0, 0, tiled=True)
+    mixed, own_grad, to_lo, to_hi, *shares = back_call(place, x, first, own, *weights)
     back_hi = along(to_lo, -1)
     back_lo = along(to_hi, 1)
-    shares = [shares[0]] + [
-        to_slot(share, dy, dx) for share, (dy, dx) in zip(shares[1:], SLOT_STEPS)
-    ]
-    cell_grad = final_call(x, dy, own_grad, back_lo, back_hi, anchor_index, face_rows, shares)
+    kept, crossing = share_call(place, spread(shares, "y"))
+    plane, kept, crossing, back_hi, back_lo = lax.optimization_barrier(
+        (plane, kept, crossing, back_hi, back_lo)
+    )
+    crossed = swapped(crossing, "xh")
+    column = plane_call(plane)
+    column = lax.all_to_all(column, "z", 0, 0, tiled=True)
+    column, own_grad = lax.optimization_barrier((column, own_grad))
+    cell_grad = final_call(
+        x, dy, own_grad, back_lo, back_hi, anchor_index, face_rows, kept, crossed
+    )
+    weight_grads = settled(place, column)
     return mixed[None], cell_grad[None], weight_grads
 
 

time: 163 us -> 114 us (0.70)
  blocking collectives: 38.3 us -> 0 us
  local copies, waits for them, and re-layouts: 37.8 us -> 0.02 us
  waiting for transfers between devices: 12.5 us -> 29.6 us
  Pallas kernels: 24.2 us -> 39.8 us
  starting transfers between devices: 45.9 us -> 42.4 us
    all_to_all x1 -> x0, blocking collectives: 38.3 us -> none  [body(): plane = lax.all_to_all(parts, PLANE, 0, 0, tiled=True)]
    unnamed x122 -> x8, local copies, waits for them, and re-layouts: 37.8 us -> 0.02 us
    ppermute x14 -> x3, starting transfers between devices: 26.1 us -> 3 us  [spread(): lax.ppermute(arrays[k], axis, [(i, (i + k) % 4) for i in range(4)])]
    all_to_all x1 -> x3, starting transfers between devices: 10.8 us -> 25.1 us  [the longest x1 9.44 us: body(): plane = lax.all_to_all(parts, ('y', 'xh', 'xl'), 0, 0, tiled=True)]
    all_to_all x1 -> x3, waiting for transfers between devices: 0.01 us -> 12 us  [the longest x1 7.75 us: body(): column = lax.all_to_all(column, 'z', 0, 0, tiled=True)]
    ppermute x14 -> x3, waiting for transfers between devices: 7.16 us -> 17.6 us  [spread(): lax.ppermute(arrays[k], axis, [(i, (i + k) % 4) for i in range(4)])]
    pallas_call x4 -> x6, Pallas kernels: 16.8 us -> 23.7 us  [the longest x1 8.99 us: attend_first_call(): pl.pallas_call(attend_first_kernel, in_specs=[smem] * 3 + [vmem] * 11, ou...]
    ppermute x1, waiting for transfers between devices: 5.32 us -> 0.01 us  [settled(): there = lax.ppermute(other, axes, swap)]
  transfers between devices with their start and end apart: 22 -> 14, of which waited for: 4 -> 6; matrix products, arithmetic and copies ran while one was open for 1% -> 0% of each run, Pallas kernels for 9% -> 21%
where the time goes in v1:
time: 114 us; the launch traced here: 113 us
  starting transfers between devices  42.4 us (37%)
  Pallas kernels  39.8 us (35%)
  waiting for transfers between devices  29.6 us (26%)
    ppermute x3, waiting for transfers between devices, spread(): lax.ppermute(arrays[k], axis, [(i, (i + k) % 4) for i in range(4)])  17.6 us
    all_to_all x1, starting transfers between devices, body(): plane = lax.all_to_all(parts, ('y', 'xh', 'xl'), 0, 0, tiled=True)  9.44 us
    pallas_call x1, Pallas kernels, attend_first_call(): pl.pallas_call(attend_first_kernel, in_specs=[smem] * 3 + [vmem] * 11, ou...  8.99 us
    all_to_all x1, starting transfers between devices, body(): column = lax.all_to_all(column, 'z', 0, 0, tiled=True)  8.47 us
    pallas_call x1, Pallas kernels, back_call(): pl.pallas_call(back_kernel, in_specs=[smem] + [vmem] * 7, out_shape=[jax....  8.31 us
    all_to_all x1, waiting for transfers between devices, body(): column = lax.all_to_all(column, 'z', 0, 0, tiled=True)  7.75 us
    all_to_all x1, starting transfers between devices, body(): anchors = lax.all_to_all(sent_anchors, SLOT, 0, 0, tiled=True)  7.15 us
    ppermute x4, starting transfers between devices, along(): return lax.ppermute(value, ('z', 'xl', 'core'), pairs)  6.9 us
  transfers between devices with their start and end apart: 14, of which 6 were waited for; matrix products, arithmetic and copies ran while one was open for 0% of the time, Pallas kernels for 21%

profile of v1, /device:TPU:24, one launch (start us, length us, event | category | flops | bytes accessed | tf_op | source)
XLA Modules:
  0.0 113.4 jit_solution(4328034455407921404)
XLA Ops:
  0.6 2.1 %shard_map.121 = (bf16[256,768]{1,0:T(8,128)(2,1)}, bf16[8,32,768]{2,1,0:T(8,128)(2,1)}, bf16[128,768]{1,0:T(8,128)(2,1)S(1)}, bf16[128,768]{1,0:T(8,128)(2,1)S(1)}) custom-call(bf16[256,768]{1,0:T(8,128)(2,1)} %bitcast.14, s32[1,32]{1,0:T(1,128)} %anchor_ref.3, s32[2,128]{1,0:T(2,128)} %bitcast.21), custom_call_target="tpu_custom_call" | custom-call | tf_op jit(solution)/shard_map/pallas_call | solution.py:66
  2.7 7.2 %all-to-all-start = ((bf16[8,32,768]{2,1,0:T(8,128)(2,1)}), bf16[8,32,768]{2,1,0:T(8,128)(2,1)S(1)}, u32[]{:S(2)}, u32[]{:S(2)}) async-start(bf16[8,32,768]{2,1,0:T(8,128)(2,1)} %get-tuple-element.41), calls=%async_computation | async-start | bytes 786432 | tf_op jit(solution)/shard_map/all_to_all | solution.py:467
  9.9 1.3 %collective-permute-start = (bf16[128,768]{1,0:T(8,128)(2,1)S(1)}, bf16[128,768]{1,0:T(8,128)(2,1)S(1)}, u32[]{:S(2)}, u32[]{:S(2)}) collective-permute-start(bf16[128,768]{1,0:T(8,128)(2,1)S(1)} %get-tuple-element.39), channel_id=1, source_target_pairs={{0,1},{1,2},{2,3},{3,4},{4,5},{5,6},{6,7},{7,8},{8,9},{9,10},{10,1... | collective-permute-start | bytes 589832 | tf_op jit(solution)/shard_map/ppermute | solution.py:393
  11.2 1.3 %collective-permute-start.1 = (bf16[128,768]{1,0:T(8,128)(2,1)S(1)}, bf16[128,768]{1,0:T(8,128)(2,1)S(1)}, u32[]{:S(2)}, u32[]{:S(2)}) collective-permute-start(bf16[128,768]{1,0:T(8,128)(2,1)S(1)} %get-tuple-element.40), channel_id=1, source_target_pairs={{1,0},{2,1},{3,2},{4,3},{5,4},{6,5},{7,6},{8,7},{9,8},{10,9},{11,1... | collective-permute-start | bytes 589832 | tf_op jit(solution)/shard_map/ppermute | solution.py:393
  12.5 4.0 %shard_map.122 = (bf16[256,768]{1,0:T(8,128)(2,1)S(1)}, bf16[256,768]{1,0:T(8,128)(2,1)S(1)}, bf16[256,768]{1,0:T(8,128)(2,1)S(1)}, bf16[256,768]{1,0:T(8,128)(2,1)S(1)}) custom-call(bf16[256,768]{1,0:T(8,128)(2,1)} %get-tuple-element.34.n_ref, bf16[256,768]{1,0:T(8,128)(2,1)} %bitcast.17, bf16[768,768]{1,0:T(8,128)(2,1)} %wq_ref.3, ...), custom_call_target="tpu_custom_call" | custom-call | tf_op jit(solution)/shard_map/pallas_call | solution.py:87
  16.5 1.6 %all-to-all-done.an_ref = bf16[8,32,768]{2,1,0:T(8,128)(2,1)S(1)} async-done(((bf16[8,32,768]{2,1,0:T(8,128)(2,1)}), bf16[8,32,768]{2,1,0:T(8,128)(2,1)S(1)}, u32[]{:S(2)}, u32[]{:S(2)}) %all-to-all-start) | async-done | bytes 393248 | tf_op jit(solution)/shard_map/all_to_all | solution.py:467
  18.1 9.0 %shard_map.123 = (bf16[2048,768]{1,0:T(8,128)(2,1)S(1)}, bf16[512,768]{1,0:T(8,128)(2,1)}) custom-call(s32[2,3]{1,0:T(2,128)S(1)} %bitcast.10, s32[2]{0:T(128)S(1)} %bitcast.12, s32[1]{0:T(128)S(6)} %sub.3.side_ref, bf16[256,768]{1,0:T(8,128)(2,1)S(1)} %get-tuple-element.35.q_ref, bf16[256,768]{1,0:T(8,128)(2,1)S(1)} %get-tuple-element.36.k_ref, ...), custom_call_target="tpu_custom_call" | custom-call | tf_op jit(solution)/shard_map/pallas_call | solution.py:204
  27.1 1.6 %collective-permute-start.2 = (bf16[2048,768]{1,0:T(8,128)(2,1)S(1)}, bf16[2048,768]{1,0:T(8,128)(2,1)S(1)}, u32[]{:S(2)}, u32[]{:S(2)}) collective-permute-start(bf16[2048,768]{1,0:T(8,128)(2,1)S(1)} %get-tuple-element.42.first_ref), channel_id=1, source_target_pairs={{0,1},{1,0},{2,3},{3,2},{4,5},{5,4},{6,7},{7,6},{8,9},{9,8},{10,11... | collective-permute-start | bytes 9437192 | tf_op jit(solution)/shard_map/ppermute | solution.py:381
  28.8 6.6 %shard_map.124.own_ref = bf16[1024,768]{1,0:T(8,128)(2,1)S(1)} custom-call(s32[2,3]{1,0:T(2,128)S(1)} %bitcast.11, s32[2]{0:T(128)S(1)} %bitcast.13, s32[1]{0:T(128)} %bitcast.2.side_ref, bf16[256,768]{1,0:T(8,128)(2,1)S(1)} %get-tuple-element.35.q_ref, bf16[256,768]{1,0:T(8,128)(2,1)S(1)} %get-tuple-element.36.k_ref, ...), custom_call_target="tpu_custom_call" | custom-call | tf_op jit(solution)/shard_map/pallas_call | solution.py:216
  35.5 4.1 %shard_map.125 = bf16[16,192,384]{2,1,0:T(8,128)(2,1)} custom-call(bf16[2048,768]{1,0:T(8,128)(2,1)S(1)} %get-tuple-element.42.first_ref, bf16[1024,768]{1,0:T(8,128)(2,1)S(1)} %shard_map.124.own_ref, bf16[2048,768]{1,0:T(8,128)(2,1)S(1)} %collective-permute-done.2.got_ref), custom_call_target="tpu_custom_call" | custom-call | tf_op jit(solution)/shard_map/pallas_call | solution.py:255
  39.6 9.4 %all-to-all-start.1 = ((bf16[16,192,384]{2,1,0:T(8,128)(2,1)}), bf16[16,192,384]{2,1,0:T(8,128)(2,1)S(1)}, u32[]{:S(2)}, u32[]{:S(2)}) async-start(bf16[16,192,384]{2,1,0:T(8,128)(2,1)} %shard_map.125), calls=%async_computation.1 | async-start | bytes 4718592 | tf_op jit(solution)/shard_map/all_to_all | solution.py:479
  49.1 8.3 %shard_map.126 = (bf16[256,768]{1,0:T(8,128)(2,1)}, f32[256,768]{1,0:T(8,128)}, bf16[128,768]{1,0:T(8,128)(2,1)S(1)}, bf16[128,768]{1,0:T(8,128)(2,1)S(1)}, bf16...) custom-call(s32[3]{0:T(128)S(1)} %pad_add_fusion.place_ref, ...), custom_call_target="tpu_custom_call" | custom-call | tf_op jit(solution)/shard_map/pallas_call | solution.py:310
  57.4 1.3 %collective-permute-start.6 = (bf16[128,768]{1,0:T(8,128)(2,1)S(1)}, bf16[128,768]{1,0:T(8,128)(2,1)S(1)}, u32[]{:S(2)}, u32[]{:S(2)}) collective-permute-start(bf16[128,768]{1,0:T(8,128)(2,1)S(1)} %get-tuple-element.53), channel_id=1, source_target_pairs={{1,0},{2,1},{3,2},{4,3},{5,4},{6,5},{7,6},{8,7},{9,8},{10,9},{11,1... | collective-permute-start | bytes 589832 | tf_op jit(solution)/shard_map/ppermute | solution.py:393
  58.7 3.0 %collective-permute-start.7 = (bf16[128,768]{1,0:T(8,128)(2,1)S(1)}, bf16[128,768]{1,0:T(8,128)(2,1)S(1)}, u32[]{:S(2)}, u32[]{:S(2)}) collective-permute-start(bf16[128,768]{1,0:T(8,128)(2,1)S(1)} %get-tuple-element.54), channel_id=1, source_target_pairs={{0,1},{1,2},{2,3},{3,4},{4,5},{5,6},{6,7},{7,8},{8,9},{9,10},{10,1... | collective-permute-start | bytes 589832 | tf_op jit(solution)/shard_map/ppermute | solution.py:393
  61.9 2.8 %collective-permute-start.4 = (bf16[64,768]{1,0:T(8,128)(2,1)S(1)}, bf16[64,768]{1,0:T(8,128)(2,1)S(1)}, u32[]{:S(2)}, u32[]{:S(2)}) collective-permute-start(bf16[64,768]{1,0:T(8,128)(2,1)S(1)} %get-tuple-element.49), channel_id=1, source_target_pairs={{0,128},{64,192},{128,0},{192,64},{1,129},{65,193},{129,1},{193,65... | collective-permute-start | bytes 294920 | tf_op jit(solution)/shard_map/ppermute | solution.py:386
  64.8 10.9 %collective-permute-done.3.s1 = bf16[64,768]{1,0:T(8,128)(2,1)S(1)} collective-permute-done((bf16[64,768]{1,0:T(8,128)(2,1)S(1)}, bf16[64,768]{1,0:T(8,128)(2,1)S(1)}, u32[]{:S(2)}, u32[]{:S(2)}) %collective-permute-start.3) | collective-permute-done | bytes 98336 | tf_op jit(solution)/shard_map/ppermute | solution.py:386
  75.6 4.9 %collective-permute-done.4.s2 = bf16[64,768]{1,0:T(8,128)(2,1)S(1)} collective-permute-done((bf16[64,768]{1,0:T(8,128)(2,1)S(1)}, bf16[64,768]{1,0:T(8,128)(2,1)S(1)}, u32[]{:S(2)}, u32[]{:S(2)}) %collective-permute-start.4) | collective-permute-done | bytes 98336 | tf_op jit(solution)/shard_map/ppermute | solution.py:386
  80.5 1.8 %collective-permute-done.5.s3 = bf16[64,768]{1,0:T(8,128)(2,1)S(1)} collective-permute-done((bf16[64,768]{1,0:T(8,128)(2,1)S(1)}, bf16[64,768]{1,0:T(8,128)(2,1)S(1)}, u32[]{:S(2)}, u32[]{:S(2)}) %collective-permute-start.5) | collective-permute-done | bytes 98336 | tf_op jit(solution)/shard_map/ppermute | solution.py:386
  83.6 2.6 %all-to-all-done.1.got_ref = bf16[16,192,384]{2,1,0:T(8,128)(2,1)S(1)} async-done(((bf16[16,192,384]{2,1,0:T(8,128)(2,1)}), bf16[16,192,384]{2,1,0:T(8,128)(2,1)S(1)}, u32[]{:S(2)}, u32[]{:S(2)}) %all-to-all-start.1) | async-done | bytes 2359328 | tf_op jit(solution)/shard_map/all_to_all | solution.py:479
  87.2 8.5 %all-to-all-start.2 = ((bf16[8,24,384]{2,1,0:T(8,128)(2,1)}), bf16[8,24,384]{2,1,0:T(8,128)(2,1)S(1)}, u32[]{:S(2)}, u32[]{:S(2)}) async-start(bf16[8,24,384]{2,1,0:T(8,128)(2,1)} %shard_map.128), calls=%async_computation.2 | async-start | bytes 294912 | tf_op jit(solution)/shard_map/all_to_all | solution.py:489
  95.7 1.8 %collective-permute-start.8 = (bf16[32,768]{1,0:T(8,128)(2,1)S(1)}, bf16[32,768]{1,0:T(8,128)(2,1)S(1)}, u32[]{:S(2)}, u32[]{:S(2)}) collective-permute-start(bf16[32,768]{1,0:T(8,128)(2,1)S(1)} %get-tuple-element.61), channel_id=1, source_target_pairs={{0,32},{32,0},{1,33},{33,1},{2,34},{34,2},{3,35},{35,3},{4,36},{36... | collective-permute-start | bytes 147464 | tf_op jit(solution)/shard_map/ppermute | solution.py:381
  97.5 7.8 %all-to-all-done.2.rows_ref = bf16[8,24,384]{2,1,0:T(8,128)(2,1)S(1)} async-done(((bf16[8,24,384]{2,1,0:T(8,128)(2,1)}), bf16[8,24,384]{2,1,0:T(8,128)(2,1)S(1)}, u32[]{:S(2)}, u32[]{:S(2)}) %all-to-all-start.2) | async-done | bytes 147488 | tf_op jit(solution)/shard_map/all_to_all | solution.py:489
  106.5 3.4 %collective-permute-start.10 = (f32[12,384]{1,0:T(8,128)S(1)}, f32[12,384]{1,0:T(8,128)S(1)}, u32[]{:S(2)}, u32[]{:S(2)}) collective-permute-start(f32[12,384]{1,0:T(8,128)S(1)} %get-tuple-element.64), channel_id=1, source_target_pairs={{192,193},{0,1},{64,65},{128,129},{193,225},{1,0},{65,64},{129,128... | collective-permute-start | bytes 55304 | tf_op jit(solution)/shard_map/ppermute | solution.py:435
  109.9 2.9 %shard_map.129 = bf16[256,768]{1,0:T(8,128)(2,1)} custom-call(bf16[256,768]{1,0:T(8,128)(2,1)} %bitcast.16, bf16[256,768]{1,0:T(8,128)(2,1)} %bitcast.19, f32[256,768]{1,0:T(8,128)} %get-tuple-element.57.own_ref, bf16[128,768]{1,0:T(8,128)(2,1)S(1)} %collective-permute-done.7.lo_ref, bf16[128,768]{1,0:T(8,128)(2,1)S(1)} %collective-permute-done.6.hi_ref, ...), custom_call_target="tpu_custom_call" | custom-call | tf_op jit(solution)/shard_map/pallas_call | solution.py:373
  (25 shorter events, 4.4 us)
Async XLA Ops:
  2.7 15.4 %all-to-all-start = ((bf16[8,32,768]{2,1,0:T(8,128)(2,1)}), bf16[8,32,768]{2,1,0:T(8,128)(2,1)S(1)}, u32[]{:S(2)}, u32[]{:S(2)}) async-start(bf16[8,32,768]{2,1,0:T(8,128)(2,1)} %get-tuple-element.41), calls=%async_computation | async-start | bytes 786432 | tf_op jit(solution)/shard_map/all_to_all | solution.py:467
  9.9 6.6 %collective-permute-start = (bf16[128,768]{1,0:T(8,128)(2,1)S(1)}, bf16[128,768]{1,0:T(8,128)(2,1)S(1)}, u32[]{:S(2)}, u32[]{:S(2)}) collective-permute-start(bf16[128,768]{1,0:T(8,128)(2,1)S(1)} %get-tuple-element.39), channel_id=1, source_target_pairs={{0,1},{1,2},{2,3},{3,4},{4,5},{5,6},{6,7},{7,8},{8,9},{9,10},{10,1... | collective-permute-start | bytes 589832 | tf_op jit(solution)/shard_map/ppermute | solution.py:393
  11.2 5.3 %collective-permute-start.1 = (bf16[128,768]{1,0:T(8,128)(2,1)S(1)}, bf16[128,768]{1,0:T(8,128)(2,1)S(1)}, u32[]{:S(2)}, u32[]{:S(2)}) collective-permute-start(bf16[128,768]{1,0:T(8,128)(2,1)S(1)} %get-tuple-element.40), channel_id=1, source_target_pairs={{1,0},{2,1},{3,2},{4,3},{5,4},{6,5},{7,6},{8,7},{9,8},{10,9},{11,1... | collective-permute-start | bytes 589832 | tf_op jit(solution)/shard_map/ppermute | solution.py:393
  12.5 5.6 %copy-start.2 = (s32[1,2,3]{2,1,0:T(2,128)S(1)}, s32[1,2,3]{2,1,0:T(2,128)}, u32[]{:S(2)}) copy-start(s32[1,2,3]{2,1,0:T(2,128)} %param.19) | copy-start | bytes 76
  12.5 5.6 %copy-start.3 = (s32[1,1,2]{2,1,0:T(1,128)S(1)}, s32[1,1,2]{2,1,0:T(1,128)}, u32[]{:S(2)}) copy-start(s32[1,1,2]{2,1,0:T(1,128)} %param.18) | copy-start | bytes 28
  27.1 8.3 %copy-start.1 = (bf16[2048,768]{1,0:T(8,128)(2,1)}, bf16[2048,768]{1,0:T(8,128)(2,1)S(1)}, u32[]{:S(2)}) copy-start(bf16[2048,768]{1,0:T(8,128)(2,1)S(1)} %get-tuple-element.42.first_ref) | copy-start | bytes 9437188
  27.1 8.3 %collective-permute-start.2 = (bf16[2048,768]{1,0:T(8,128)(2,1)S(1)}, bf16[2048,768]{1,0:T(8,128)(2,1)S(1)}, u32[]{:S(2)}, u32[]{:S(2)}) collective-permute-start(bf16[2048,768]{1,0:T(8,128)(2,1)S(1)} %get-tuple-element.42.first_ref), channel_id=1, source_target_pairs={{0,1},{1,0},{2,3},{3,2},{4,5},{5,4},{6,7},{7,6},{8,9},{9,8},{10,11... | collective-permute-start | bytes 9437192 | tf_op jit(solution)/shard_map/ppermute | solution.py:381
  35.4 4.2 %copy-start = (bf16[1024,768]{1,0:T(8,128)(2,1)}, bf16[1024,768]{1,0:T(8,128)(2,1)S(1)}, u32[]{:S(2)}) copy-start(bf16[1024,768]{1,0:T(8,128)(2,1)S(1)} %shard_map.124.own_ref) | copy-start | bytes 4718596
  39.6 46.6 %all-to-all-start.1 = ((bf16[16,192,384]{2,1,0:T(8,128)(2,1)}), bf16[16,192,384]{2,1,0:T(8,128)(2,1)S(1)}, u32[]{:S(2)}, u32[]{:S(2)}) async-start(bf16[16,192,384]{2,1,0:T(8,128)(2,1)} %shard_map.125), calls=%async_computation.1 | async-start | bytes 4718592 | tf_op jit(solution)/shard_map/all_to_all | solution.py:479
  57.4 26.2 %collective-permute-start.6 = (bf16[128,768]{1,0:T(8,128)(2,1)S(1)}, bf16[128,768]{1,0:T(8,128)(2,1)S(1)}, u32[]{:S(2)}, u32[]{:S(2)}) collective-permute-start(bf16[128,768]{1,0:T(8,128)(2,1)S(1)} %get-tuple-element.53), channel_id=1, source_target_pairs={{1,0},{2,1},{3,2},{4,3},{5,4},{6,5},{7,6},{8,7},{9,8},{10,9},{11,1... | collective-permute-start | bytes 589832 | tf_op jit(solution)/shard_map/ppermute | solution.py:393
  58.7 24.9 %collective-permute-start.7 = (bf16[128,768]{1,0:T(8,128)(2,1)S(1)}, bf16[128,768]{1,0:T(8,128)(2,1)S(1)}, u32[]{:S(2)}, u32[]{:S(2)}) collective-permute-start(bf16[128,768]{1,0:T(8,128)(2,1)S(1)} %get-tuple-element.54), channel_id=1, source_target_pairs={{0,1},{1,2},{2,3},{3,4},{4,5},{5,6},{6,7},{7,8},{8,9},{9,10},{10,1... | collective-permute-start | bytes 589832 | tf_op jit(solution)/shard_map/ppermute | solution.py:393
  61.8 13.9 %collective-permute-start.3 = (bf16[64,768]{1,0:T(8,128)(2,1)S(1)}, bf16[64,768]{1,0:T(8,128)(2,1)S(1)}, u32[]{:S(2)}, u32[]{:S(2)}) collective-permute-start(bf16[64,768]{1,0:T(8,128)(2,1)S(1)} %get-tuple-element.48), channel_id=1, source_target_pairs={{0,64},{64,128},{128,192},{192,0},{1,65},{65,129},{129,193},{193,1... | collective-permute-start | bytes 294920 | tf_op jit(solution)/shard_map/ppermute | solution.py:386
  61.9 18.6 %collective-permute-start.4 = (bf16[64,768]{1,0:T(8,128)(2,1)S(1)}, bf16[64,768]{1,0:T(8,128)(2,1)S(1)}, u32[]{:S(2)}, u32[]{:S(2)}) collective-permute-start(bf16[64,768]{1,0:T(8,128)(2,1)S(1)} %get-tuple-element.49), channel_id=1, source_target_pairs={{0,128},{64,192},{128,0},{192,64},{1,129},{65,193},{129,1},{193,65... | collective-permute-start | bytes 294920 | tf_op jit(solution)/shard_map/ppermute | solution.py:386
  64.8 17.6 %collective-permute-start.5 = (bf16[64,768]{1,0:T(8,128)(2,1)S(1)}, bf16[64,768]{1,0:T(8,128)(2,1)S(1)}, u32[]{:S(2)}, u32[]{:S(2)}) collective-permute-start(bf16[64,768]{1,0:T(8,128)(2,1)S(1)} %get-tuple-element.50), channel_id=1, source_target_pairs={{0,192},{64,0},{128,64},{192,128},{1,193},{65,1},{129,65},{193,129... | collective-permute-start | bytes 294920 | tf_op jit(solution)/shard_map/ppermute | solution.py:386
  87.2 18.0 %all-to-all-start.2 = ((bf16[8,24,384]{2,1,0:T(8,128)(2,1)}), bf16[8,24,384]{2,1,0:T(8,128)(2,1)S(1)}, u32[]{:S(2)}, u32[]{:S(2)}) async-start(bf16[8,24,384]{2,1,0:T(8,128)(2,1)} %shard_map.128), calls=%async_computation.2 | async-start | bytes 294912 | tf_op jit(solution)/shard_map/all_to_all | solution.py:489
  95.7 14.2 %collective-permute-start.8 = (bf16[32,768]{1,0:T(8,128)(2,1)S(1)}, bf16[32,768]{1,0:T(8,128)(2,1)S(1)}, u32[]{:S(2)}, u32[]{:S(2)}) collective-permute-start(bf16[32,768]{1,0:T(8,128)(2,1)S(1)} %get-tuple-element.61), channel_id=1, source_target_pairs={{0,32},{32,0},{1,33},{33,1},{2,34},{34,2},{3,35},{35,3},{4,36},{36... | collective-permute-start | bytes 147464 | tf_op jit(solution)/shard_map/ppermute | solution.py:381
  105.8 6.9 %collective-permute-start.9 = (f32[12,384]{1,0:T(8,128)S(1)}, f32[12,384]{1,0:T(8,128)S(1)}, u32[]{:S(2)}, u32[]{:S(2)}) collective-permute-start(f32[12,384]{1,0:T(8,128)S(1)} %get-tuple-element.63), channel_id=1, source_target_pairs={{192,192},{193,224},{224,193},{225,225},{194,194},{195,226},{226,1... | collective-permute-start | bytes 55304 | tf_op jit(solution)/shard_map/ppermute | solution.py:433
  106.5 6.3 %collective-permute-start.10 = (f32[12,384]{1,0:T(8,128)S(1)}, f32[12,384]{1,0:T(8,128)S(1)}, u32[]{:S(2)}, u32[]{:S(2)}) collective-permute-start(f32[12,384]{1,0:T(8,128)S(1)} %get-tuple-element.64), channel_id=1, source_target_pairs={{192,193},{0,1},{64,65},{128,129},{193,225},{1,0},{65,64},{129,128... | collective-permute-start | bytes 55304 | tf_op jit(solution)/shard_map/ppermute | solution.py:435

commit v2 on v1

--- a/solution.py
+++ b/solution.py
@@ -226,8 +226,8 @@
     mine = slice(1024, 1024 + KEY_ROWS)
 
     def block(term, low, cols):
-        rows = [term[m + 24 * low:m + 24 * low + 24, cols] for m in range(0, term.shape[0], 48)]
-        return jnp.concatenate(rows, 0).astype(bf16)
+        starts = [48 * z + 24 * low for odd in range(2) for z in range(odd, 8, 2)]
+        return jnp.concatenate([term[m:m + 24, cols] for m in starts], 0).astype(bf16)
 
     def keep(matrix, term, cols):
         for high in range(2):
@@ -260,15 +260,15 @@
 
 
 def plane_kernel(got_ref, out_ref):
-    result = total([got_ref[index] for index in range(16)])
-    for z in range(8):
+    result = total([got_ref[index] for index in range(32)])
+    for z in range(4):
         out_ref[z] = result[24 * z:24 * z + 24].astype(bf16)
 
 
 def plane_call(got):
     return pl.pallas_call(
         plane_kernel,
-        out_shape=jax.ShapeDtypeStruct((8, 24, SIDE), bf16),
+        out_shape=jax.ShapeDtypeStruct((4, 24, SIDE), bf16),
         compiler_params=params(10),
     )(got)
 
@@ -280,43 +280,69 @@
     return result
 
 
-def back_kernel(place_ref, x_ref, first_ref, own_ref, wq_ref, wk_ref, wv_ref, wo_ref,
-                mixed_ref, ng_ref, lo_ref, hi_ref, a0_ref, a1_ref, a2_ref, a3_ref, rows):
-    core = place_ref[2]
-    kv = None
-    extra = None
-    out = x_ref[...].astype(f32)
-    for source, side in ((own_ref, core), (first_ref, 1 - core)):
-        half = pl.ds(pl.multiple_of(side * SIDE, SIDE), SIDE)
-        term = dot(source[CELLS:1024, :SIDE], wk_ref[:, half], NT)
-        kv = term if kv is None else kv + term
-        kv = kv + dot(source[CELLS:1024, SIDE:], wv_ref[:, half], NT)
-        term = dot(source[0:CELLS, SIDE:], wq_ref[:, half], NT)
-        extra = term if extra is None else extra + term
-        out = out + dot(source[0:CELLS, :SIDE], wo_ref[half, :])
-    ng_ref[...] = kv[:CELLS] + extra
+def started(pairs, sems):
+    copies = [pltpu.make_async_copy(src, dst, sems.at[i]) for i, (src, dst) in enumerate(pairs)]
+    for copy in copies:
+        copy.start()
+    return copies
+
+
+def waited(copies):
+    for copy in copies:
+        copy.wait()
+
+
+def halves(core):
+    return [pl.ds(pl.multiple_of(side * SIDE, SIDE), SIDE) for side in (core, 1 - core)]
+
+
+def back_kernel(place_ref, x_ref, first_any, own_any, wq_any, wk_any, wv_any, wo_any, mixed_ref,
+                ng_ref, lo_ref, hi_ref, a0_ref, a1_ref, a2_ref, a3_ref, rows, own_ref, first_ref,
+                wq_ref, wk_ref, wv_ref, wo_ref, sems):
+    loads = started(
+        [
+            (wk_any, wk_ref), (own_any, own_ref), (wv_any, wv_ref),
+            (first_any.at[0:1024, :], first_ref), (wq_any, wq_ref), (wo_any, wo_ref),
+        ],
+        sems,
+    )
+    sources = list(zip((own_ref, first_ref), halves(place_ref[2])))
+    waited(loads[:2])
+    kv = dot(own_ref[CELLS:, :SIDE], wk_ref[:, sources[0][1]], NT)
+    waited(loads[2:3])
+    kv = kv + dot(own_ref[CELLS:, SIDE:], wv_ref[:, sources[0][1]], NT)
+    waited(loads[3:])
+    kv = kv + dot(first_ref[CELLS:, :SIDE], wk_ref[:, sources[1][1]], NT)
+    kv = kv + dot(first_ref[CELLS:, SIDE:], wv_ref[:, sources[1][1]], NT)
     lo_ref[...] = kv[CELLS:CELLS + BS].astype(bf16)
     hi_ref[...] = kv[CELLS + BS:POOL_ROWS].astype(bf16)
     for y in range(4):
         rows[y] = kv[POOL_ROWS + 64 * y:POOL_ROWS + 64 * y + 64].astype(bf16)
     for step, target in enumerate((a0_ref, a1_ref, a2_ref, a3_ref)):
         target[...] = rows[(place_ref[1] + step) % 4]
+    grad = kv[:CELLS]
+    out = x_ref[...].astype(f32)
+    for source, half in sources:
+        grad = grad + dot(source[:CELLS, SIDE:], wq_ref[:, half], NT)
+        out = out + dot(source[:CELLS, :SIDE], wo_ref[half, :])
+    ng_ref[...] = grad
     mixed_ref[...] = out.astype(bf16)
 
 
 def back_call(place, x, first, own, wq, wk, wv, wo):
     smem = pl.BlockSpec(memory_space=pltpu.SMEM)
-    vmem = pl.BlockSpec(memory_space=pltpu.VMEM)
+    whole = pl.BlockSpec(memory_space=pltpu.VMEM)
+    anywhere = pl.BlockSpec(memory_space=pl.ANY)
     return pl.pallas_call(
         back_kernel,
-        in_specs=[smem] + [vmem] * 7,
-        out_shape=[
-            jax.ShapeDtypeStruct((CELLS, D), bf16),
-            pltpu.HBM((CELLS, D), f32),
-            jax.ShapeDtypeStruct((BS, D), bf16),
-            jax.ShapeDtypeStruct((BS, D), bf16),
-        ] + [jax.ShapeDtypeStruct((64, D), bf16)] * 4,
-        scratch_shapes=[pltpu.VMEM((4, 64, D), bf16)],
+        in_specs=[smem, whole] + [anywhere] * 6,
+        out_shape=[jax.ShapeDtypeStruct((CELLS, D), bf16), pltpu.HBM((CELLS, D), f32)]
+        + [jax.ShapeDtypeStruct((BS, D), bf16)] * 2
+        + [jax.ShapeDtypeStruct((64, D), bf16)] * 4,
+        scratch_shapes=[pltpu.VMEM((4, 64, D), bf16)]
+        + [pltpu.VMEM((1024, D), bf16)] * 2
+        + [pltpu.VMEM((D, D), bf16)] * 4
+        + [pltpu.SemaphoreType.DMA((6,))],
         compiler_params=params(24),
     )(place, *held(x, first, own, wq, wk, wv, wo))
 
@@ -390,7 +416,7 @@
 def along(value, step):
     count = 32
     pairs = [(i, i + step) for i in range(count) if 0 <= i + step < count]
-    return lax.ppermute(value, ("z", "xl", "core"), pairs)
+    return lax.ppermute(value, ("zh", "zl", "xl", "core"), pairs)
 
 
 X_RING = ("xh", "xl")
@@ -398,7 +424,7 @@
 
 
 def settle_kernel(place_ref, rows_ref, own_ref, other_ref):
-    rows = total([rows_ref[index] for index in range(8)])
+    rows = total([rows_ref[index] for index in range(4)])
     upper = jnp.where(place_ref[1] == 3, place_ref[0] // 2, place_ref[2]) == 1
     own_ref[...] = jnp.where(upper, rows[12:], rows[:12])
     other_ref[...] = jnp.where(upper, rows[:12], rows[12:])
@@ -476,17 +502,17 @@
 
     parts = outer_call(first, own, got)
     own, parts = lax.optimization_barrier((own, parts))
-    plane = lax.all_to_all(parts, ("y", "xh", "xl"), 0, 0, tiled=True)
+    plane = lax.all_to_all(parts.reshape(32, 96, SIDE), ("y", "xh", "xl", "zl"), 0, 0, tiled=True)
     mixed, own_grad, to_lo, to_hi, *shares = back_call(place, x, first, own, *weights)
+    shares = spread(shares, "y")
     back_hi = along(to_lo, -1)
     back_lo = along(to_hi, 1)
-    kept, crossing = share_call(place, spread(shares, "y"))
-    plane, kept, crossing, back_hi, back_lo = lax.optimization_barrier(
-        (plane, kept, crossing, back_hi, back_lo)
-    )
+    plane, shares[1] = lax.optimization_barrier((plane, shares[1]))
+    kept, crossing = share_call(place, shares)
     crossed = swapped(crossing, "xh")
     column = plane_call(plane)
-    column = lax.all_to_all(column, "z", 0, 0, tiled=True)
+    column, back_hi, back_lo = lax.optimization_barrier((column, back_hi, back_lo))
+    column = lax.all_to_all(column, "zh", 0, 0, tiled=True)
     column, own_grad = lax.optimization_barrier((column, own_grad))
     cell_grad = final_call(
         x, dy, own_grad, back_lo, back_hi, anchor_index, face_rows, kept, crossed
@@ -496,8 +522,8 @@
 
 
 def solution(mesh):
-    fine = Mesh(mesh.devices.reshape(4, 2, 8, 2, 2), ("y", "xh", "z", "xl", "core"))
-    dom = ("z", "xl", "core")
+    fine = Mesh(mesh.devices.reshape(4, 2, 4, 2, 2, 2), ("y", "xh", "zh", "zl", "xl", "core"))
+    dom = ("zh", "zl", "xl", "core")
     blk = ("y", "xh")
     return jax.shard_map(
         body,

time: 114 us -> 111 us (0.974)
  the two profiles are of different devices: /device:TPU:24 before, /device:TPU:59 now
where the time goes in v2:
time: 111 us; the launch traced here: 110 us
  starting transfers between devices  52.9 us (48%)
  Pallas kernels  40 us (36%)
  waiting for transfers between devices  15.4 us (14%)
    ppermute x4, starting transfers between devices, along(): return lax.ppermute(value, ('zh', 'zl', 'xl', 'core'), pairs)  16.1 us
    ppermute x3, waiting for transfers between devices, spread(): lax.ppermute(arrays[k], axis, [(i, (i + k) % 4) for i in range(4)])  10.3 us
    pallas_call x1, Pallas kernels, attend_first_call(): pl.pallas_call(attend_first_kernel, in_specs=[smem] * 3 + [vmem] * 11, ou...  8.98 us
    ppermute x1, starting transfers between devices, settled(): turned = lax.ppermute(own, axes, turn)  8.79 us
    pallas_call x1, Pallas kernels, back_call(): pl.pallas_call(back_kernel, in_specs=[smem, whole] + [anywhere] * 6, out_...  7.87 us
    all_to_all x1, starting transfers between devices, body(): lax.all_to_all(parts.reshape(32, 96, SIDE), ('y', 'xh', 'xl', 'zl'), 0, 0...  7.77 us
    pallas_call x1, Pallas kernels, attend_second_call(): pl.pallas_call(attend_second_kernel, in_specs=[smem] * 3 + [vmem] * 5, ou...  7.25 us
    all_to_all x1, starting transfers between devices, body(): column = lax.all_to_all(column, 'zh', 0, 0, tiled=True)  6.86 us
  transfers between devices with their start and end apart: 14, of which 4 were waited for; matrix products, arithmetic and copies ran while one was open for 0% of the time, Pallas kernels for 23%

profile of v2, /device:TPU:59, one launch (start us, length us, event | category | flops | bytes accessed | tf_op | source)
XLA Modules:
  0.0 109.9 jit_solution(2205851033285599995)
XLA Ops:
  0.6 2.1 %shard_map.121 = (bf16[256,768]{1,0:T(8,128)(2,1)}, bf16[8,32,768]{2,1,0:T(8,128)(2,1)}, bf16[128,768]{1,0:T(8,128)(2,1)S(1)}, bf16[128,768]{1,0:T(8,128)(2,1)S(1)}) custom-call(bf16[256,768]{1,0:T(8,128)(2,1)} %bitcast.16, s32[1,32]{1,0:T(1,128)} %anchor_ref.3, s32[2,128]{1,0:T(2,128)} %bitcast.23), custom_call_target="tpu_custom_call" | custom-call | tf_op jit(solution)/shard_map/pallas_call | solution.py:66
  2.7 5.7 %all-to-all-start = ((bf16[8,32,768]{2,1,0:T(8,128)(2,1)}), bf16[8,32,768]{2,1,0:T(8,128)(2,1)S(1)}, u32[]{:S(2)}, u32[]{:S(2)}) async-start(bf16[8,32,768]{2,1,0:T(8,128)(2,1)} %get-tuple-element.41), calls=%async_computation | async-start | bytes 786432 | tf_op jit(solution)/shard_map/all_to_all | solution.py:493
  8.4 5.5 %collective-permute-start = (bf16[128,768]{1,0:T(8,128)(2,1)S(1)}, bf16[128,768]{1,0:T(8,128)(2,1)S(1)}, u32[]{:S(2)}, u32[]{:S(2)}) collective-permute-start(bf16[128,768]{1,0:T(8,128)(2,1)S(1)} %get-tuple-element.39), channel_id=1, source_target_pairs={{0,1},{1,2},{2,3},{3,4},{4,5},{5,6},{6,7},{7,8},{8,9},{9,10},{10,1... | collective-permute-start | bytes 589832 | tf_op jit(solution)/shard_map/ppermute | solution.py:419
  14.0 1.9 %collective-permute-start.1 = (bf16[128,768]{1,0:T(8,128)(2,1)S(1)}, bf16[128,768]{1,0:T(8,128)(2,1)S(1)}, u32[]{:S(2)}, u32[]{:S(2)}) collective-permute-start(bf16[128,768]{1,0:T(8,128)(2,1)S(1)} %get-tuple-element.40), channel_id=1, source_target_pairs={{1,0},{2,1},{3,2},{4,3},{5,4},{6,5},{7,6},{8,7},{9,8},{10,9},{11,1... | collective-permute-start | bytes 589832 | tf_op jit(solution)/shard_map/ppermute | solution.py:419
  15.9 4.0 %shard_map.122 = (bf16[256,768]{1,0:T(8,128)(2,1)S(1)}, bf16[256,768]{1,0:T(8,128)(2,1)S(1)}, bf16[256,768]{1,0:T(8,128)(2,1)S(1)}, bf16[256,768]{1,0:T(8,128)(2,1)S(1)}) custom-call(bf16[256,768]{1,0:T(8,128)(2,1)} %get-tuple-element.34.n_ref, bf16[256,768]{1,0:T(8,128)(2,1)} %bitcast.19, bf16[768,768]{1,0:T(8,128)(2,1)} %wq_any.1, ...), custom_call_target="tpu_custom_call" | custom-call | tf_op jit(solution)/shard_map/pallas_call | solution.py:87
  19.9 1.9 %collective-permute-done.1.hi_ref = bf16[128,768]{1,0:T(8,128)(2,1)S(1)} collective-permute-done((bf16[128,768]{1,0:T(8,128)(2,1)S(1)}, bf16[128,768]{1,0:T(8,128)(2,1)S(1)}, u32[]{:S(2)}, u32[]{:S(2)}) %collective-permute-start.1) | collective-permute-done | bytes 196640 | tf_op jit(solution)/shard_map/ppermute | solution.py:419
  21.9 9.0 %shard_map.123 = (bf16[2048,768]{1,0:T(8,128)(2,1)S(1)}, bf16[512,768]{1,0:T(8,128)(2,1)}) custom-call(s32[2,3]{1,0:T(2,128)S(1)} %bitcast.11, s32[2]{0:T(128)S(1)} %bitcast.13, s32[1]{0:T(128)S(6)} %sub.3.side_ref, bf16[256,768]{1,0:T(8,128)(2,1)S(1)} %get-tuple-element.35.q_ref, bf16[256,768]{1,0:T(8,128)(2,1)S(1)} %get-tuple-element.36.k_ref, ...), custom_call_target="tpu_custom_call" | custom-call | tf_op jit(solution)/shard_map/pallas_call | solution.py:204
  31.1 7.2 %shard_map.124.own_ref.own_any = bf16[1024,768]{1,0:T(8,128)(2,1)S(1)} custom-call(s32[2,3]{1,0:T(2,128)S(1)} %bitcast.12, s32[2]{0:T(128)S(1)} %bitcast.14, s32[1]{0:T(128)} %bitcast.2.side_ref, bf16[256,768]{1,0:T(8,128)(2,1)S(1)} %get-tuple-element.35.q_ref, bf16[256,768]{1,0:T(8,128)(2,1)S(1)} %get-tuple-element.36.k_ref, ...), custom_call_target="tpu_custom_call" | custom-call | tf_op jit(solution)/shard_map/pallas_call | solution.py:216
  38.4 4.1 %shard_map.125 = bf16[16,192,384]{2,1,0:T(8,128)(2,1)} custom-call(bf16[2048,768]{1,0:T(8,128)(2,1)S(1)} %get-tuple-element.42.first_ref.first_any, bf16[1024,768]{1,0:T(8,128)(2,1)S(1)} %shard_map.124.own_ref.own_any, bf16[2048,768]{1,0:T(8,128)(2,1)S(1)} %collective-permute-done.2.got_ref), custom_call_target="tpu_custom_call" | custom-call | tf_op jit(solution)/shard_map/pallas_call | solution.py:255
  42.6 7.8 %all-to-all-start.1 = ((bf16[32,96,384]{2,1,0:T(8,128)(2,1)}), bf16[32,96,384]{2,1,0:T(8,128)(2,1)S(1)}, u32[]{:S(2)}, u32[]{:S(2)}) async-start(bf16[32,96,384]{2,1,0:T(8,128)(2,1)} %bitcast.15), calls=%async_computation.1 | async-start | bytes 4718592 | tf_op jit(solution)/shard_map/all_to_all | solution.py:505
  50.4 7.9 %shard_map.126 = (bf16[256,768]{1,0:T(8,128)(2,1)}, f32[256,768]{1,0:T(8,128)}, bf16[128,768]{1,0:T(8,128)(2,1)S(1)}, bf16[128,768]{1,0:T(8,128)(2,1)S(1)}, bf16...) custom-call(s32[3]{0:T(128)S(1)} %pad_add_fusion.place_ref, ...), custom_call_target="tpu_custom_call" | custom-call | tf_op jit(solution)/shard_map/pallas_call | solution.py:336
  58.3 2.3 %collective-permute-start.4 = (bf16[128,768]{1,0:T(8,128)(2,1)S(1)}, bf16[128,768]{1,0:T(8,128)(2,1)S(1)}, u32[]{:S(2)}, u32[]{:S(2)}) collective-permute-start(bf16[128,768]{1,0:T(8,128)(2,1)S(1)} %get-tuple-element.49), channel_id=1, source_target_pairs={{1,0},{2,1},{3,2},{4,3},{5,4},{6,5},{7,6},{8,7},{9,8},{10,9},{11,1... | collective-permute-start | bytes 589832 | tf_op jit(solution)/shard_map/ppermute | solution.py:419
  60.7 6.3 %collective-permute-start.5 = (bf16[128,768]{1,0:T(8,128)(2,1)S(1)}, bf16[128,768]{1,0:T(8,128)(2,1)S(1)}, u32[]{:S(2)}, u32[]{:S(2)}) collective-permute-start(bf16[128,768]{1,0:T(8,128)(2,1)S(1)} %get-tuple-element.50), channel_id=1, source_target_pairs={{0,1},{1,2},{2,3},{3,4},{4,5},{5,6},{6,7},{7,8},{8,9},{9,10},{10,1... | collective-permute-start | bytes 589832 | tf_op jit(solution)/shard_map/ppermute | solution.py:419
  67.1 2.3 %collective-permute-start.6 = (bf16[64,768]{1,0:T(8,128)(2,1)}, bf16[64,768]{1,0:T(8,128)(2,1)S(1)}, u32[]{:S(2)}, u32[]{:S(2)}) collective-permute-start(bf16[64,768]{1,0:T(8,128)(2,1)} %get-tuple-element.58), channel_id=1, source_target_pairs={{0,128},{64,192},{128,0},{192,64},{1,129},{65,193},{129,1},{193,65... | collective-permute-start | bytes 294920 | tf_op jit(solution)/shard_map/ppermute | solution.py:412
  69.4 10.3 %collective-permute-done.3.s1 = bf16[64,768]{1,0:T(8,128)(2,1)S(1)} collective-permute-done((bf16[64,768]{1,0:T(8,128)(2,1)S(1)}, bf16[64,768]{1,0:T(8,128)(2,1)S(1)}, u32[]{:S(2)}, u32[]{:S(2)}) %collective-permute-start.3) | collective-permute-done | bytes 98336 | tf_op jit(solution)/shard_map/ppermute | solution.py:412
  79.7 2.4 %all-to-all-done.1.got_ref = bf16[32,96,384]{2,1,0:T(8,128)(2,1)S(1)} async-done(((bf16[32,96,384]{2,1,0:T(8,128)(2,1)}), bf16[32,96,384]{2,1,0:T(8,128)(2,1)S(1)}, u32[]{:S(2)}, u32[]{:S(2)}) %all-to-all-start.1) | async-done | bytes 2359328 | tf_op jit(solution)/shard_map/all_to_all | solution.py:505
  82.1 1.0 shard_map.127
  83.1 6.9 %all-to-all-start.2 = ((bf16[4,24,384]{2,1,0:T(8,128)(2,1)}), bf16[4,24,384]{2,1,0:T(8,128)(2,1)S(1)}, u32[]{:S(2)}, u32[]{:S(2)}) async-start(bf16[4,24,384]{2,1,0:T(8,128)(2,1)} %shard_map.127), calls=%async_computation.2 | async-start | bytes 147456 | tf_op jit(solution)/shard_map/all_to_all | solution.py:515
  90.0 1.2 %shard_map.128 = (f32[32,768]{1,0:T(8,128)}, bf16[32,768]{1,0:T(8,128)(2,1)S(1)}) custom-call(s32[3]{0:T(128)S(1)} %pad_add_fusion.place_ref, bf16[64,768]{1,0:T(8,128)(2,1)S(1)} %get-tuple-element.56.s0, bf16[64,768]{1,0:T(8,128)(2,1)S(1)} %collective-permute-done.3.s1, bf16[64,768]{1,0:T(8,128)(2,1)S(1)} %collective-permute-done.6.s2, ...), custom_call_target="tpu_custom_call" | custom-call | tf_op jit(solution)/shard_map/pallas_call | solution.py:362
  91.2 4.9 %collective-permute-start.8 = (bf16[32,768]{1,0:T(8,128)(2,1)S(1)}, bf16[32,768]{1,0:T(8,128)(2,1)S(1)}, u32[]{:S(2)}, u32[]{:S(2)}) collective-permute-start(bf16[32,768]{1,0:T(8,128)(2,1)S(1)} %get-tuple-element.61), channel_id=1, source_target_pairs={{0,32},{32,0},{1,33},{33,1},{2,34},{34,2},{3,35},{35,3},{4,36},{36... | collective-permute-start | bytes 147464 | tf_op jit(solution)/shard_map/ppermute | solution.py:407
  96.1 0.8 all-to-all-done.2.rows_ref
  97.4 8.8 %collective-permute-start.9 = (f32[12,384]{1,0:T(8,128)S(1)}, f32[12,384]{1,0:T(8,128)S(1)}, u32[]{:S(2)}, u32[]{:S(2)}) collective-permute-start(f32[12,384]{1,0:T(8,128)S(1)} %get-tuple-element.63), channel_id=1, source_target_pairs={{192,192},{193,224},{224,193},{225,225},{194,194},{195,226},{226,1... | collective-permute-start | bytes 55304 | tf_op jit(solution)/shard_map/ppermute | solution.py:459
  106.4 2.9 %shard_map.129 = bf16[256,768]{1,0:T(8,128)(2,1)} custom-call(bf16[256,768]{1,0:T(8,128)(2,1)} %bitcast.18, bf16[256,768]{1,0:T(8,128)(2,1)} %bitcast.21, f32[256,768]{1,0:T(8,128)} %get-tuple-element.53.own_ref, bf16[128,768]{1,0:T(8,128)(2,1)S(1)} %collective-permute-done.5.lo_ref, bf16[128,768]{1,0:T(8,128)(2,1)S(1)} %collective-permute-done.4.hi_ref, ...), custom_call_target="tpu_custom_call" | custom-call | tf_op jit(solution)/shard_map/pallas_call | solution.py:399
  109.3 0.6 maximum_select_fusion
  (25 shorter events, 1.2 us)
Async XLA Ops:
  2.7 19.1 %all-to-all-start = ((bf16[8,32,768]{2,1,0:T(8,128)(2,1)}), bf16[8,32,768]{2,1,0:T(8,128)(2,1)S(1)}, u32[]{:S(2)}, u32[]{:S(2)}) async-start(bf16[8,32,768]{2,1,0:T(8,128)(2,1)} %get-tuple-element.41), calls=%async_computation | async-start | bytes 786432 | tf_op jit(solution)/shard_map/all_to_all | solution.py:493
  8.4 11.5 %collective-permute-start = (bf16[128,768]{1,0:T(8,128)(2,1)S(1)}, bf16[128,768]{1,0:T(8,128)(2,1)S(1)}, u32[]{:S(2)}, u32[]{:S(2)}) collective-permute-start(bf16[128,768]{1,0:T(8,128)(2,1)S(1)} %get-tuple-element.39), channel_id=1, source_target_pairs={{0,1},{1,2},{2,3},{3,4},{4,5},{5,6},{6,7},{7,8},{8,9},{9,10},{10,1... | collective-permute-start | bytes 589832 | tf_op jit(solution)/shard_map/ppermute | solution.py:419
  14.0 7.9 %collective-permute-start.1 = (bf16[128,768]{1,0:T(8,128)(2,1)S(1)}, bf16[128,768]{1,0:T(8,128)(2,1)S(1)}, u32[]{:S(2)}, u32[]{:S(2)}) collective-permute-start(bf16[128,768]{1,0:T(8,128)(2,1)S(1)} %get-tuple-element.40), channel_id=1, source_target_pairs={{1,0},{2,1},{3,2},{4,3},{5,4},{6,5},{7,6},{8,7},{9,8},{10,9},{11,1... | collective-permute-start | bytes 589832 | tf_op jit(solution)/shard_map/ppermute | solution.py:419
  15.9 6.0 %copy-start.2 = (s32[1,2,3]{2,1,0:T(2,128)S(1)}, s32[1,2,3]{2,1,0:T(2,128)}, u32[]{:S(2)}) copy-start(s32[1,2,3]{2,1,0:T(2,128)} %param.19) | copy-start | bytes 76
  15.9 6.0 %copy-start.3 = (s32[1,1,2]{2,1,0:T(1,128)S(1)}, s32[1,1,2]{2,1,0:T(1,128)}, u32[]{:S(2)}) copy-start(s32[1,1,2]{2,1,0:T(1,128)} %param.18) | copy-start | bytes 28
  30.9 7.6 %copy-start.1 = (bf16[2048,768]{1,0:T(8,128)(2,1)}, bf16[2048,768]{1,0:T(8,128)(2,1)S(1)}, u32[]{:S(2)}) copy-start(bf16[2048,768]{1,0:T(8,128)(2,1)S(1)} %get-tuple-element.42.first_ref.first_any) | copy-start | bytes 9437188
  30.9 7.6 %collective-permute-start.2 = (bf16[2048,768]{1,0:T(8,128)(2,1)S(1)}, bf16[2048,768]{1,0:T(8,128)(2,1)S(1)}, u32[]{:S(2)}, u32[]{:S(2)}) collective-permute-start(bf16[2048,768]{1,0:T(8,128)(2,1)S(1)} %get-tuple-element.42.first_ref.first_any), channel_id=1, source_target_pairs={{0,1},{1,0},{2,3},{3,2},{4,5},{5,4},{6,7},{7,6},{8,9},{9,8},{10,11... | collective-permute-start | bytes 9437192 | tf_op jit(solution)/shard_map/ppermute | solution.py:407
  38.4 4.2 %copy-start = (bf16[1024,768]{1,0:T(8,128)(2,1)}, bf16[1024,768]{1,0:T(8,128)(2,1)S(1)}, u32[]{:S(2)}) copy-start(bf16[1024,768]{1,0:T(8,128)(2,1)S(1)} %shard_map.124.own_ref.own_any) | copy-start | bytes 4718596
  42.6 39.5 %all-to-all-start.1 = ((bf16[32,96,384]{2,1,0:T(8,128)(2,1)}), bf16[32,96,384]{2,1,0:T(8,128)(2,1)S(1)}, u32[]{:S(2)}, u32[]{:S(2)}) async-start(bf16[32,96,384]{2,1,0:T(8,128)(2,1)} %bitcast.15), calls=%async_computation.1 | async-start | bytes 4718592 | tf_op jit(solution)/shard_map/all_to_all | solution.py:505
  58.3 24.8 %collective-permute-start.4 = (bf16[128,768]{1,0:T(8,128)(2,1)S(1)}, bf16[128,768]{1,0:T(8,128)(2,1)S(1)}, u32[]{:S(2)}, u32[]{:S(2)}) collective-permute-start(bf16[128,768]{1,0:T(8,128)(2,1)S(1)} %get-tuple-element.49), channel_id=1, source_target_pairs={{1,0},{2,1},{3,2},{4,3},{5,4},{6,5},{7,6},{8,7},{9,8},{10,9},{11,1... | collective-permute-start | bytes 589832 | tf_op jit(solution)/shard_map/ppermute | solution.py:419
  60.7 22.4 %collective-permute-start.5 = (bf16[128,768]{1,0:T(8,128)(2,1)S(1)}, bf16[128,768]{1,0:T(8,128)(2,1)S(1)}, u32[]{:S(2)}, u32[]{:S(2)}) collective-permute-start(bf16[128,768]{1,0:T(8,128)(2,1)S(1)} %get-tuple-element.50), channel_id=1, source_target_pairs={{0,1},{1,2},{2,3},{3,4},{4,5},{5,6},{6,7},{7,8},{8,9},{9,10},{10,1... | collective-permute-start | bytes 589832 | tf_op jit(solution)/shard_map/ppermute | solution.py:419
  67.0 12.7 %collective-permute-start.3 = (bf16[64,768]{1,0:T(8,128)(2,1)S(1)}, bf16[64,768]{1,0:T(8,128)(2,1)S(1)}, u32[]{:S(2)}, u32[]{:S(2)}) collective-permute-start(bf16[64,768]{1,0:T(8,128)(2,1)S(1)} %get-tuple-element.47), channel_id=1, source_target_pairs={{0,64},{64,128},{128,192},{192,0},{1,65},{65,129},{129,193},{193,1... | collective-permute-start | bytes 294920 | tf_op jit(solution)/shard_map/ppermute | solution.py:412
  67.1 22.9 %collective-permute-start.6 = (bf16[64,768]{1,0:T(8,128)(2,1)}, bf16[64,768]{1,0:T(8,128)(2,1)S(1)}, u32[]{:S(2)}, u32[]{:S(2)}) collective-permute-start(bf16[64,768]{1,0:T(8,128)(2,1)} %get-tuple-element.58), channel_id=1, source_target_pairs={{0,128},{64,192},{128,0},{192,64},{1,129},{65,193},{129,1},{193,65... | collective-permute-start | bytes 294920 | tf_op jit(solution)/shard_map/ppermute | solution.py:412
  69.4 20.5 %collective-permute-start.7 = (bf16[64,768]{1,0:T(8,128)(2,1)}, bf16[64,768]{1,0:T(8,128)(2,1)S(1)}, u32[]{:S(2)}, u32[]{:S(2)}) collective-permute-start(bf16[64,768]{1,0:T(8,128)(2,1)} %get-tuple-element.59), channel_id=1, source_target_pairs={{0,192},{64,0},{128,64},{192,128},{1,193},{65,1},{129,65},{193,129... | collective-permute-start | bytes 294920 | tf_op jit(solution)/shard_map/ppermute | solution.py:412
  83.1 13.8 %all-to-all-start.2 = ((bf16[4,24,384]{2,1,0:T(8,128)(2,1)}), bf16[4,24,384]{2,1,0:T(8,128)(2,1)S(1)}, u32[]{:S(2)}, u32[]{:S(2)}) async-start(bf16[4,24,384]{2,1,0:T(8,128)(2,1)} %shard_map.127), calls=%async_computation.2 | async-start | bytes 147456 | tf_op jit(solution)/shard_map/all_to_all | solution.py:515
  91.2 15.2 %collective-permute-start.8 = (bf16[32,768]{1,0:T(8,128)(2,1)S(1)}, bf16[32,768]{1,0:T(8,128)(2,1)S(1)}, u32[]{:S(2)}, u32[]{:S(2)}) collective-permute-start(bf16[32,768]{1,0:T(8,128)(2,1)S(1)} %get-tuple-element.61), channel_id=1, source_target_pairs={{0,32},{32,0},{1,33},{33,1},{2,34},{34,2},{3,35},{35,3},{4,36},{36... | collective-permute-start | bytes 147464 | tf_op jit(solution)/shard_map/ppermute | solution.py:407
  97.4 11.8 %collective-permute-start.9 = (f32[12,384]{1,0:T(8,128)S(1)}, f32[12,384]{1,0:T(8,128)S(1)}, u32[]{:S(2)}, u32[]{:S(2)}) collective-permute-start(f32[12,384]{1,0:T(8,128)S(1)} %get-tuple-element.63), channel_id=1, source_target_pairs={{192,192},{193,224},{224,193},{225,225},{194,194},{195,226},{226,1... | collective-permute-start | bytes 55304 | tf_op jit(solution)/shard_map/ppermute | solution.py:459
  106.2 3.0 %collective-permute-start.10 = (f32[12,384]{1,0:T(8,128)S(1)}, f32[12,384]{1,0:T(8,128)S(1)}, u32[]{:S(2)}, u32[]{:S(2)}) collective-permute-start(f32[12,384]{1,0:T(8,128)S(1)} %get-tuple-element.64), channel_id=1, source_target_pairs={{192,193},{0,1},{64,65},{128,129},{193,225},{1,0},{65,64},{129,128... | collective-permute-start | bytes 55304 | tf_op jit(solution)/shard_map/ppermute | solution.py:461

commit v3 on v2

--- a/solution.py
+++ b/solution.py
@@ -229,10 +229,14 @@
         starts = [48 * z + 24 * low for odd in range(2) for z in range(odd, 8, 2)]
         return jnp.concatenate([term[m:m + 24, cols] for m in starts], 0).astype(bf16)
 
+    def put(slot, rows):
+        parts[0, slot] = rows[:96]
+        parts[1, slot] = rows[96:]
+
     def keep(matrix, term, cols):
         for high in range(2):
             for low in range(2):
-                parts[4 * matrix + 2 * high + low] = block(term[high * SIDE:(high + 1) * SIDE], low, cols)
+                put(4 * matrix + 2 * high + low, block(term[high * SIDE:(high + 1) * SIDE], low, cols))
 
     left, right = slice(0, SIDE), slice(SIDE, D)
     keep(0, dot(first_ref[mine, :CELLS], own_ref[0:CELLS, right])
@@ -248,13 +252,13 @@
     )
     for high in range(2):
         for low in range(2):
-            parts[12 + 2 * high + low] = block(out_term, low, right if high else left)
+            put(12 + 2 * high + low, block(out_term, low, right if high else left))
 
 
 def outer_call(first, own, got):
     return pl.pallas_call(
         outer_kernel,
-        out_shape=pltpu.HBM((16, 192, SIDE), bf16),
+        out_shape=pltpu.HBM((2, 16, 96, SIDE), bf16),
         compiler_params=params(32),
     )(first, own, got)
 
@@ -502,12 +506,12 @@
 
     parts = outer_call(first, own, got)
     own, parts = lax.optimization_barrier((own, parts))
-    plane = lax.all_to_all(parts.reshape(32, 96, SIDE), ("y", "xh", "xl", "zl"), 0, 0, tiled=True)
+    plane = lax.all_to_all(parts.reshape(32, 96, SIDE), ("zl", "y", "xh", "xl"), 0, 0, tiled=True)
     mixed, own_grad, to_lo, to_hi, *shares = back_call(place, x, first, own, *weights)
     shares = spread(shares, "y")
     back_hi = along(to_lo, -1)
     back_lo = along(to_hi, 1)
-    plane, shares[1] = lax.optimization_barrier((plane, shares[1]))
+    plane, back_hi = lax.optimization_barrier((plane, back_hi))
     kept, crossing = share_call(place, shares)
     crossed = swapped(crossing, "xh")
     column = plane_call(plane)

time: 111 us -> 108 us (0.973)
  the two profiles are of different devices: /device:TPU:59 before, /device:TPU:24 now
where the time goes in v3:
time: 108 us
  starting transfers between devices  44 us (41%)
  Pallas kernels  39.4 us (36%)
  waiting for transfers between devices  22.8 us (21%)
    all_to_all x1, waiting for transfers between devices, body(): lax.all_to_all(parts.reshape(32, 96, SIDE), ('zl', 'y', 'xh', 'xl'), 0, 0...  16.2 us
    all_to_all x1, starting transfers between devices, body(): lax.all_to_all(parts.reshape(32, 96, SIDE), ('zl', 'y', 'xh', 'xl'), 0, 0...  10.9 us
    pallas_call x1, Pallas kernels, attend_first_call(): pl.pallas_call(attend_first_kernel, in_specs=[smem] * 3 + [vmem] * 11, ou...  8.99 us
    pallas_call x1, Pallas kernels, back_call(): pl.pallas_call(back_kernel, in_specs=[smem, whole] + [anywhere] * 6, out_...  7.88 us
    all_to_all x1, starting transfers between devices, body(): column = lax.all_to_all(column, 'zh', 0, 0, tiled=True)  7.47 us
    all_to_all x1, starting transfers between devices, body(): anchors = lax.all_to_all(sent_anchors, SLOT, 0, 0, tiled=True)  7.15 us
    ppermute x4, starting transfers between devices, along(): return lax.ppermute(value, ('zh', 'zl', 'xl', 'core'), pairs)  6.92 us
    pallas_call x1, Pallas kernels, attend_second_call(): pl.pallas_call(attend_second_kernel, in_specs=[smem] * 3 + [vmem] * 5, ou...  6.64 us
  transfers between devices with their start and end apart: 14, of which 3 were waited for; matrix products, arithmetic and copies ran while one was open for 0% of the time, Pallas kernels for 22%

profile of v3, /device:TPU:24, one launch (start us, length us, event | category | flops | bytes accessed | tf_op | source)
XLA Modules:
  0.0 107.7 jit_solution(4442510840963101839)
XLA Ops:
  0.6 2.1 %shard_map.121 = (bf16[256,768]{1,0:T(8,128)(2,1)}, bf16[8,32,768]{2,1,0:T(8,128)(2,1)}, bf16[128,768]{1,0:T(8,128)(2,1)S(1)}, bf16[128,768]{1,0:T(8,128)(2,1)S(1)}) custom-call(bf16[256,768]{1,0:T(8,128)(2,1)} %bitcast.16, s32[1,32]{1,0:T(1,128)} %anchor_ref.3, s32[2,128]{1,0:T(2,128)} %bitcast.23), custom_call_target="tpu_custom_call" | custom-call | tf_op jit(solution)/shard_map/pallas_call | solution.py:66
  2.7 7.2 %all-to-all-start = ((bf16[8,32,768]{2,1,0:T(8,128)(2,1)}), bf16[8,32,768]{2,1,0:T(8,128)(2,1)S(1)}, u32[]{:S(2)}, u32[]{:S(2)}) async-start(bf16[8,32,768]{2,1,0:T(8,128)(2,1)} %get-tuple-element.41), calls=%async_computation | async-start | bytes 786432 | tf_op jit(solution)/shard_map/all_to_all | solution.py:497
  9.9 1.3 %collective-permute-start = (bf16[128,768]{1,0:T(8,128)(2,1)S(1)}, bf16[128,768]{1,0:T(8,128)(2,1)S(1)}, u32[]{:S(2)}, u32[]{:S(2)}) collective-permute-start(bf16[128,768]{1,0:T(8,128)(2,1)S(1)} %get-tuple-element.39), channel_id=1, source_target_pairs={{0,1},{1,2},{2,3},{3,4},{4,5},{5,6},{6,7},{7,8},{8,9},{9,10},{10,1... | collective-permute-start | bytes 589832 | tf_op jit(solution)/shard_map/ppermute | solution.py:423
  11.2 1.3 %collective-permute-start.1 = (bf16[128,768]{1,0:T(8,128)(2,1)S(1)}, bf16[128,768]{1,0:T(8,128)(2,1)S(1)}, u32[]{:S(2)}, u32[]{:S(2)}) collective-permute-start(bf16[128,768]{1,0:T(8,128)(2,1)S(1)} %get-tuple-element.40), channel_id=1, source_target_pairs={{1,0},{2,1},{3,2},{4,3},{5,4},{6,5},{7,6},{8,7},{9,8},{10,9},{11,1... | collective-permute-start | bytes 589832 | tf_op jit(solution)/shard_map/ppermute | solution.py:423
  12.5 4.0 %shard_map.122 = (bf16[256,768]{1,0:T(8,128)(2,1)S(1)}, bf16[256,768]{1,0:T(8,128)(2,1)S(1)}, bf16[256,768]{1,0:T(8,128)(2,1)S(1)}, bf16[256,768]{1,0:T(8,128)(2,1)S(1)}) custom-call(bf16[256,768]{1,0:T(8,128)(2,1)} %get-tuple-element.34.n_ref, bf16[256,768]{1,0:T(8,128)(2,1)} %bitcast.19, bf16[768,768]{1,0:T(8,128)(2,1)} %wq_any.1, ...), custom_call_target="tpu_custom_call" | custom-call | tf_op jit(solution)/shard_map/pallas_call | solution.py:87
  16.5 1.6 %all-to-all-done.an_ref = bf16[8,32,768]{2,1,0:T(8,128)(2,1)S(1)} async-done(((bf16[8,32,768]{2,1,0:T(8,128)(2,1)}), bf16[8,32,768]{2,1,0:T(8,128)(2,1)S(1)}, u32[]{:S(2)}, u32[]{:S(2)}) %all-to-all-start) | async-done | bytes 393248 | tf_op jit(solution)/shard_map/all_to_all | solution.py:497
  18.1 9.0 %shard_map.123 = (bf16[2048,768]{1,0:T(8,128)(2,1)S(1)}, bf16[512,768]{1,0:T(8,128)(2,1)}) custom-call(s32[2,3]{1,0:T(2,128)S(1)} %bitcast.11, s32[2]{0:T(128)S(1)} %bitcast.13, s32[1]{0:T(128)S(6)} %sub.3.side_ref, bf16[256,768]{1,0:T(8,128)(2,1)S(1)} %get-tuple-element.35.q_ref, bf16[256,768]{1,0:T(8,128)(2,1)S(1)} %get-tuple-element.36.k_ref, ...), custom_call_target="tpu_custom_call" | custom-call | tf_op jit(solution)/shard_map/pallas_call | solution.py:204
  27.1 1.6 %collective-permute-start.2 = (bf16[2048,768]{1,0:T(8,128)(2,1)S(1)}, bf16[2048,768]{1,0:T(8,128)(2,1)S(1)}, u32[]{:S(2)}, u32[]{:S(2)}) collective-permute-start(bf16[2048,768]{1,0:T(8,128)(2,1)S(1)} %get-tuple-element.42.first_ref.first_any), channel_id=1, source_target_pairs={{0,1},{1,0},{2,3},{3,2},{4,5},{5,4},{6,7},{7,6},{8,9},{9,8},{10,11... | collective-permute-start | bytes 9437192 | tf_op jit(solution)/shard_map/ppermute | solution.py:411
  28.8 6.6 %shard_map.124.own_ref.own_any = bf16[1024,768]{1,0:T(8,128)(2,1)S(1)} custom-call(s32[2,3]{1,0:T(2,128)S(1)} %bitcast.12, s32[2]{0:T(128)S(1)} %bitcast.14, s32[1]{0:T(128)} %bitcast.2.side_ref, bf16[256,768]{1,0:T(8,128)(2,1)S(1)} %get-tuple-element.35.q_ref, bf16[256,768]{1,0:T(8,128)(2,1)S(1)} %get-tuple-element.36.k_ref, ...), custom_call_target="tpu_custom_call" | custom-call | tf_op jit(solution)/shard_map/pallas_call | solution.py:216
  35.5 4.1 %shard_map.125 = bf16[2,16,96,384]{3,2,1,0:T(8,128)(2,1)} custom-call(bf16[2048,768]{1,0:T(8,128)(2,1)S(1)} %get-tuple-element.42.first_ref.first_any, bf16[1024,768]{1,0:T(8,128)(2,1)S(1)} %shard_map.124.own_ref.own_any, bf16[2048,768]{1,0:T(8,128)(2,1)S(1)} %collective-permute-done.2.got_ref), custom_call_target="tpu_custom_call" | custom-call | tf_op jit(solution)/shard_map/pallas_call | solution.py:259
  39.6 10.9 %all-to-all-start.1 = ((bf16[32,96,384]{2,1,0:T(8,128)(2,1)}), bf16[32,96,384]{2,1,0:T(8,128)(2,1)S(1)}, u32[]{:S(2)}, u32[]{:S(2)}) async-start(bf16[32,96,384]{2,1,0:T(8,128)(2,1)} %bitcast.15), calls=%async_computation.1 | async-start | bytes 4718592 | tf_op jit(solution)/shard_map/all_to_all | solution.py:509
  50.6 7.9 %shard_map.126 = (bf16[256,768]{1,0:T(8,128)(2,1)}, f32[256,768]{1,0:T(8,128)}, bf16[128,768]{1,0:T(8,128)(2,1)S(1)}, bf16[128,768]{1,0:T(8,128)(2,1)S(1)}, bf16...) custom-call(s32[3]{0:T(128)S(1)} %pad_add_fusion.place_ref, ...), custom_call_target="tpu_custom_call" | custom-call | tf_op jit(solution)/shard_map/pallas_call | solution.py:340
  58.5 1.3 %collective-permute-start.3 = (bf16[128,768]{1,0:T(8,128)(2,1)S(1)}, bf16[128,768]{1,0:T(8,128)(2,1)S(1)}, u32[]{:S(2)}, u32[]{:S(2)}) collective-permute-start(bf16[128,768]{1,0:T(8,128)(2,1)S(1)} %get-tuple-element.47), channel_id=1, source_target_pairs={{1,0},{2,1},{3,2},{4,3},{5,4},{6,5},{7,6},{8,7},{9,8},{10,9},{11,1... | collective-permute-start | bytes 589832 | tf_op jit(solution)/shard_map/ppermute | solution.py:423
  59.8 3.0 %collective-permute-start.4 = (bf16[128,768]{1,0:T(8,128)(2,1)S(1)}, bf16[128,768]{1,0:T(8,128)(2,1)S(1)}, u32[]{:S(2)}, u32[]{:S(2)}) collective-permute-start(bf16[128,768]{1,0:T(8,128)(2,1)S(1)} %get-tuple-element.50), channel_id=1, source_target_pairs={{0,1},{1,2},{2,3},{3,4},{4,5},{5,6},{6,7},{7,8},{8,9},{9,10},{10,1... | collective-permute-start | bytes 589832 | tf_op jit(solution)/shard_map/ppermute | solution.py:423
  63.2 2.7 %collective-permute-start.6 = (bf16[64,768]{1,0:T(8,128)(2,1)S(1)}, bf16[64,768]{1,0:T(8,128)(2,1)S(1)}, u32[]{:S(2)}, u32[]{:S(2)}) collective-permute-start(bf16[64,768]{1,0:T(8,128)(2,1)S(1)} %get-tuple-element.58), channel_id=1, source_target_pairs={{0,128},{64,192},{128,0},{192,64},{1,129},{65,193},{129,1},{193,65... | collective-permute-start | bytes 294920 | tf_op jit(solution)/shard_map/ppermute | solution.py:416
  65.9 16.2 %all-to-all-done.1.got_ref = bf16[32,96,384]{2,1,0:T(8,128)(2,1)S(1)} async-done(((bf16[32,96,384]{2,1,0:T(8,128)(2,1)}), bf16[32,96,384]{2,1,0:T(8,128)(2,1)S(1)}, u32[]{:S(2)}, u32[]{:S(2)}) %all-to-all-start.1) | async-done | bytes 2359328 | tf_op jit(solution)/shard_map/all_to_all | solution.py:509
  82.1 1.0 shard_map.127
  83.0 7.5 %all-to-all-start.2 = ((bf16[4,24,384]{2,1,0:T(8,128)(2,1)}), bf16[4,24,384]{2,1,0:T(8,128)(2,1)S(1)}, u32[]{:S(2)}, u32[]{:S(2)}) async-start(bf16[4,24,384]{2,1,0:T(8,128)(2,1)} %shard_map.127), calls=%async_computation.2 | async-start | bytes 147456 | tf_op jit(solution)/shard_map/all_to_all | solution.py:519
  90.5 1.2 %shard_map.128 = (f32[32,768]{1,0:T(8,128)}, bf16[32,768]{1,0:T(8,128)(2,1)S(1)}) custom-call(s32[3]{0:T(128)S(1)} %pad_add_fusion.place_ref, bf16[64,768]{1,0:T(8,128)(2,1)S(1)} %get-tuple-element.56.s0, bf16[64,768]{1,0:T(8,128)(2,1)S(1)} %collective-permute-done.5.s1, bf16[64,768]{1,0:T(8,128)(2,1)S(1)} %collective-permute-done.6.s2, ...), custom_call_target="tpu_custom_call" | custom-call | tf_op jit(solution)/shard_map/pallas_call | solution.py:366
  91.8 2.1 %collective-permute-start.8 = (bf16[32,768]{1,0:T(8,128)(2,1)S(1)}, bf16[32,768]{1,0:T(8,128)(2,1)S(1)}, u32[]{:S(2)}, u32[]{:S(2)}) collective-permute-start(bf16[32,768]{1,0:T(8,128)(2,1)S(1)} %get-tuple-element.61), channel_id=1, source_target_pairs={{0,32},{32,0},{1,33},{33,1},{2,34},{34,2},{3,35},{35,3},{4,36},{36... | collective-permute-start | bytes 147464 | tf_op jit(solution)/shard_map/ppermute | solution.py:411
  93.9 4.9 %all-to-all-done.2.rows_ref = bf16[4,24,384]{2,1,0:T(8,128)(2,1)S(1)} async-done(((bf16[4,24,384]{2,1,0:T(8,128)(2,1)}), bf16[4,24,384]{2,1,0:T(8,128)(2,1)S(1)}, u32[]{:S(2)}, u32[]{:S(2)}) %all-to-all-start.2) | async-done | bytes 73760 | tf_op jit(solution)/shard_map/all_to_all | solution.py:519
  99.4 0.7 collective-permute-start.9
  100.0 4.1 %collective-permute-start.10 = (f32[12,384]{1,0:T(8,128)S(1)}, f32[12,384]{1,0:T(8,128)S(1)}, u32[]{:S(2)}, u32[]{:S(2)}) collective-permute-start(f32[12,384]{1,0:T(8,128)S(1)} %get-tuple-element.64), channel_id=1, source_target_pairs={{192,193},{0,1},{64,65},{128,129},{193,225},{1,0},{65,64},{129,128... | collective-permute-start | bytes 55304 | tf_op jit(solution)/shard_map/ppermute | solution.py:465
  104.2 2.9 %shard_map.129 = bf16[256,768]{1,0:T(8,128)(2,1)} custom-call(bf16[256,768]{1,0:T(8,128)(2,1)} %bitcast.18, bf16[256,768]{1,0:T(8,128)(2,1)} %bitcast.21, f32[256,768]{1,0:T(8,128)} %get-tuple-element.53.own_ref, bf16[128,768]{1,0:T(8,128)(2,1)S(1)} %collective-permute-done.4.lo_ref, bf16[128,768]{1,0:T(8,128)(2,1)S(1)} %collective-permute-done.3.hi_ref, ...), custom_call_target="tpu_custom_call" | custom-call | tf_op jit(solution)/shard_map/pallas_call | solution.py:403
  (25 shorter events, 1.6 us)
Async XLA Ops:
  2.7 15.4 %all-to-all-start = ((bf16[8,32,768]{2,1,0:T(8,128)(2,1)}), bf16[8,32,768]{2,1,0:T(8,128)(2,1)S(1)}, u32[]{:S(2)}, u32[]{:S(2)}) async-start(bf16[8,32,768]{2,1,0:T(8,128)(2,1)} %get-tuple-element.41), calls=%async_computation | async-start | bytes 786432 | tf_op jit(solution)/shard_map/all_to_all | solution.py:497
  9.9 6.6 %collective-permute-start = (bf16[128,768]{1,0:T(8,128)(2,1)S(1)}, bf16[128,768]{1,0:T(8,128)(2,1)S(1)}, u32[]{:S(2)}, u32[]{:S(2)}) collective-permute-start(bf16[128,768]{1,0:T(8,128)(2,1)S(1)} %get-tuple-element.39), channel_id=1, source_target_pairs={{0,1},{1,2},{2,3},{3,4},{4,5},{5,6},{6,7},{7,8},{8,9},{9,10},{10,1... | collective-permute-start | bytes 589832 | tf_op jit(solution)/shard_map/ppermute | solution.py:423
  11.2 5.3 %collective-permute-start.1 = (bf16[128,768]{1,0:T(8,128)(2,1)S(1)}, bf16[128,768]{1,0:T(8,128)(2,1)S(1)}, u32[]{:S(2)}, u32[]{:S(2)}) collective-permute-start(bf16[128,768]{1,0:T(8,128)(2,1)S(1)} %get-tuple-element.40), channel_id=1, source_target_pairs={{1,0},{2,1},{3,2},{4,3},{5,4},{6,5},{7,6},{8,7},{9,8},{10,9},{11,1... | collective-permute-start | bytes 589832 | tf_op jit(solution)/shard_map/ppermute | solution.py:423
  12.5 5.6 %copy-start.2 = (s32[1,2,3]{2,1,0:T(2,128)S(1)}, s32[1,2,3]{2,1,0:T(2,128)}, u32[]{:S(2)}) copy-start(s32[1,2,3]{2,1,0:T(2,128)} %param.19) | copy-start | bytes 76
  12.5 5.6 %copy-start.3 = (s32[1,1,2]{2,1,0:T(1,128)S(1)}, s32[1,1,2]{2,1,0:T(1,128)}, u32[]{:S(2)}) copy-start(s32[1,1,2]{2,1,0:T(1,128)} %param.18) | copy-start | bytes 28
  27.1 8.3 %copy-start.1 = (bf16[2048,768]{1,0:T(8,128)(2,1)}, bf16[2048,768]{1,0:T(8,128)(2,1)S(1)}, u32[]{:S(2)}) copy-start(bf16[2048,768]{1,0:T(8,128)(2,1)S(1)} %get-tuple-element.42.first_ref.first_any) | copy-start | bytes 9437188
  27.1 8.3 %collective-permute-start.2 = (bf16[2048,768]{1,0:T(8,128)(2,1)S(1)}, bf16[2048,768]{1,0:T(8,128)(2,1)S(1)}, u32[]{:S(2)}, u32[]{:S(2)}) collective-permute-start(bf16[2048,768]{1,0:T(8,128)(2,1)S(1)} %get-tuple-element.42.first_ref.first_any), channel_id=1, source_target_pairs={{0,1},{1,0},{2,3},{3,2},{4,5},{5,4},{6,7},{7,6},{8,9},{9,8},{10,11... | collective-permute-start | bytes 9437192 | tf_op jit(solution)/shard_map/ppermute | solution.py:411
  35.4 4.2 %copy-start = (bf16[1024,768]{1,0:T(8,128)(2,1)}, bf16[1024,768]{1,0:T(8,128)(2,1)S(1)}, u32[]{:S(2)}) copy-start(bf16[1024,768]{1,0:T(8,128)(2,1)S(1)} %shard_map.124.own_ref.own_any) | copy-start | bytes 4718596
  39.6 42.5 %all-to-all-start.1 = ((bf16[32,96,384]{2,1,0:T(8,128)(2,1)}), bf16[32,96,384]{2,1,0:T(8,128)(2,1)S(1)}, u32[]{:S(2)}, u32[]{:S(2)}) async-start(bf16[32,96,384]{2,1,0:T(8,128)(2,1)} %bitcast.15), calls=%async_computation.1 | async-start | bytes 4718592 | tf_op jit(solution)/shard_map/all_to_all | solution.py:509
  58.5 7.4 %collective-permute-start.3 = (bf16[128,768]{1,0:T(8,128)(2,1)S(1)}, bf16[128,768]{1,0:T(8,128)(2,1)S(1)}, u32[]{:S(2)}, u32[]{:S(2)}) collective-permute-start(bf16[128,768]{1,0:T(8,128)(2,1)S(1)} %get-tuple-element.47), channel_id=1, source_target_pairs={{1,0},{2,1},{3,2},{4,3},{5,4},{6,5},{7,6},{8,7},{9,8},{10,9},{11,1... | collective-permute-start | bytes 589832 | tf_op jit(solution)/shard_map/ppermute | solution.py:423
  59.8 23.2 %collective-permute-start.4 = (bf16[128,768]{1,0:T(8,128)(2,1)S(1)}, bf16[128,768]{1,0:T(8,128)(2,1)S(1)}, u32[]{:S(2)}, u32[]{:S(2)}) collective-permute-start(bf16[128,768]{1,0:T(8,128)(2,1)S(1)} %get-tuple-element.50), channel_id=1, source_target_pairs={{0,1},{1,2},{2,3},{3,4},{4,5},{5,6},{6,7},{7,8},{8,9},{9,10},{10,1... | collective-permute-start | bytes 589832 | tf_op jit(solution)/shard_map/ppermute | solution.py:423
  62.9 27.7 %collective-permute-start.5 = (bf16[64,768]{1,0:T(8,128)(2,1)}, bf16[64,768]{1,0:T(8,128)(2,1)S(1)}, u32[]{:S(2)}, u32[]{:S(2)}) collective-permute-start(bf16[64,768]{1,0:T(8,128)(2,1)} %get-tuple-element.57), channel_id=1, source_target_pairs={{0,64},{64,128},{128,192},{192,0},{1,65},{65,129},{129,193},{193,1... | collective-permute-start | bytes 294920 | tf_op jit(solution)/shard_map/ppermute | solution.py:416
  63.2 27.4 %collective-permute-start.6 = (bf16[64,768]{1,0:T(8,128)(2,1)S(1)}, bf16[64,768]{1,0:T(8,128)(2,1)S(1)}, u32[]{:S(2)}, u32[]{:S(2)}) collective-permute-start(bf16[64,768]{1,0:T(8,128)(2,1)S(1)} %get-tuple-element.58), channel_id=1, source_target_pairs={{0,128},{64,192},{128,0},{192,64},{1,129},{65,193},{129,1},{193,65... | collective-permute-start | bytes 294920 | tf_op jit(solution)/shard_map/ppermute | solution.py:416
  65.9 24.7 %collective-permute-start.7 = (bf16[64,768]{1,0:T(8,128)(2,1)S(1)}, bf16[64,768]{1,0:T(8,128)(2,1)S(1)}, u32[]{:S(2)}, u32[]{:S(2)}) collective-permute-start(bf16[64,768]{1,0:T(8,128)(2,1)S(1)} %get-tuple-element.59), channel_id=1, source_target_pairs={{0,192},{64,0},{128,64},{192,128},{1,193},{65,1},{129,65},{193,129... | collective-permute-start | bytes 294920 | tf_op jit(solution)/shard_map/ppermute | solution.py:416
  83.0 15.7 %all-to-all-start.2 = ((bf16[4,24,384]{2,1,0:T(8,128)(2,1)}), bf16[4,24,384]{2,1,0:T(8,128)(2,1)S(1)}, u32[]{:S(2)}, u32[]{:S(2)}) async-start(bf16[4,24,384]{2,1,0:T(8,128)(2,1)} %shard_map.127), calls=%async_computation.2 | async-start | bytes 147456 | tf_op jit(solution)/shard_map/all_to_all | solution.py:519
  91.8 12.4 %collective-permute-start.8 = (bf16[32,768]{1,0:T(8,128)(2,1)S(1)}, bf16[32,768]{1,0:T(8,128)(2,1)S(1)}, u32[]{:S(2)}, u32[]{:S(2)}) collective-permute-start(bf16[32,768]{1,0:T(8,128)(2,1)S(1)} %get-tuple-element.61), channel_id=1, source_target_pairs={{0,32},{32,0},{1,33},{33,1},{2,34},{34,2},{3,35},{35,3},{4,36},{36... | collective-permute-start | bytes 147464 | tf_op jit(solution)/shard_map/ppermute | solution.py:411
  99.4 7.7 %collective-permute-start.9 = (f32[12,384]{1,0:T(8,128)S(1)}, f32[12,384]{1,0:T(8,128)S(1)}, u32[]{:S(2)}, u32[]{:S(2)}) collective-permute-start(f32[12,384]{1,0:T(8,128)S(1)} %get-tuple-element.63), channel_id=1, source_target_pairs={{192,192},{193,224},{224,193},{225,225},{194,194},{195,226},{226,1... | collective-permute-start | bytes 55304 | tf_op jit(solution)/shard_map/ppermute | solution.py:463
  100.0 7.0 %collective-permute-start.10 = (f32[12,384]{1,0:T(8,128)S(1)}, f32[12,384]{1,0:T(8,128)S(1)}, u32[]{:S(2)}, u32[]{:S(2)}) collective-permute-start(f32[12,384]{1,0:T(8,128)S(1)} %get-tuple-element.64), channel_id=1, source_target_pairs={{192,193},{0,1},{64,65},{128,129},{193,225},{1,0},{65,64},{129,128... | collective-permute-start | bytes 55304 | tf_op jit(solution)/shard_map/ppermute | solution.py:465

commit v4 on v2

--- a/solution.py
+++ b/solution.py
@@ -19,6 +19,7 @@
 SIDE = 384
 PAIRS = 3
 SLOTS = 8
+WIDE = (("zl", 2), ("xh", 2), ("y", 4), ("xl", 2))
 PAIR = 128
 SCALE = 0.125
 EPSILON = 1e-06
@@ -229,10 +230,18 @@
         starts = [48 * z + 24 * low for odd in range(2) for z in range(odd, 8, 2)]
         return jnp.concatenate([term[m:m + 24, cols] for m in starts], 0).astype(bf16)
 
+    def put(matrix, high, low, rows):
+        place = {"y": matrix, "xh": high, "xl": low}
+        for odd in range(2):
+            slot = 0
+            for axis, size in WIDE:
+                slot = slot * size + (odd if axis == "zl" else place[axis])
+            parts[slot] = rows[96 * odd:96 * odd + 96]
+
     def keep(matrix, term, cols):
         for high in range(2):
             for low in range(2):
-                parts[4 * matrix + 2 * high + low] = block(term[high * SIDE:(high + 1) * SIDE], low, cols)
+                put(matrix, high, low, block(term[high * SIDE:(high + 1) * SIDE], low, cols))
 
     left, right = slice(0, SIDE), slice(SIDE, D)
     keep(0, dot(first_ref[mine, :CELLS], own_ref[0:CELLS, right])
@@ -248,13 +257,13 @@
     )
     for high in range(2):
         for low in range(2):
-            parts[12 + 2 * high + low] = block(out_term, low, right if high else left)
+            put(3, high, low, block(out_term, low, right if high else left))
 
 
 def outer_call(first, own, got):
     return pl.pallas_call(
         outer_kernel,
-        out_shape=pltpu.HBM((16, 192, SIDE), bf16),
+        out_shape=pltpu.HBM((32, 96, SIDE), bf16),
         compiler_params=params(32),
     )(first, own, got)
 
@@ -502,12 +511,12 @@
 
     parts = outer_call(first, own, got)
     own, parts = lax.optimization_barrier((own, parts))
-    plane = lax.all_to_all(parts.reshape(32, 96, SIDE), ("y", "xh", "xl", "zl"), 0, 0, tiled=True)
+    plane = lax.all_to_all(parts, tuple(axis for axis, _ in WIDE), 0, 0, tiled=True)
     mixed, own_grad, to_lo, to_hi, *shares = back_call(place, x, first, own, *weights)
     shares = spread(shares, "y")
     back_hi = along(to_lo, -1)
     back_lo = along(to_hi, 1)
-    plane, shares[1] = lax.optimization_barrier((plane, shares[1]))
+    plane, back_hi = lax.optimization_barrier((plane, back_hi))
     kept, crossing = share_call(place, shares)
     crossed = swapped(crossing, "xh")
     column = plane_call(plane)

time: 111 us -> 112 us (level)
  the two profiles are of different devices: /device:TPU:59 before, /device:TPU:24 now
where the time goes in v4:
time: 112 us; the launch traced here: 111 us
  starting transfers between devices  50 us (45%)
  Pallas kernels  39.4 us (35%)
  waiting for transfers between devices  20.4 us (18%)
    all_to_all x1, waiting for transfers between devices, body(): lax.all_to_all(parts, tuple((axis for axis, _ in WIDE)), 0, 0, tiled=True)  17.4 us
    all_to_all x1, starting transfers between devices, body(): lax.all_to_all(parts, tuple((axis for axis, _ in WIDE)), 0, 0, tiled=True)  10.9 us
    pallas_call x1, Pallas kernels, attend_first_call(): pl.pallas_call(attend_first_kernel, in_specs=[smem] * 3 + [vmem] * 11, ou...  8.99 us
    pallas_call x1, Pallas kernels, back_call(): pl.pallas_call(back_kernel, in_specs=[smem, whole] + [anywhere] * 6, out_...  7.88 us
    ppermute x2, starting transfers between devices, swapped(): return lax.ppermute(value, axis, [(0, 1), (1, 0)])  7.3 us
    all_to_all x1, starting transfers between devices, body(): anchors = lax.all_to_all(sent_anchors, SLOT, 0, 0, tiled=True)  7.15 us
    ppermute x1, starting transfers between devices, settled(): there = lax.ppermute(other, axes, swap)  7.13 us
    ppermute x4, starting transfers between devices, along(): return lax.ppermute(value, ('zh', 'zl', 'xl', 'core'), pairs)  6.92 us
  transfers between devices with their start and end apart: 14, of which 3 were waited for; matrix products, arithmetic and copies ran while one was open for 0% of the time, Pallas kernels for 22%

profile of v4, /device:TPU:24, one launch (start us, length us, event | category | flops | bytes accessed | tf_op | source)
XLA Modules:
  0.0 111.3 jit_solution(6104722884846646694)
XLA Ops:
  0.6 2.1 %shard_map.121 = (bf16[256,768]{1,0:T(8,128)(2,1)}, bf16[8,32,768]{2,1,0:T(8,128)(2,1)}, bf16[128,768]{1,0:T(8,128)(2,1)S(1)}, bf16[128,768]{1,0:T(8,128)(2,1)S(1)}) custom-call(bf16[256,768]{1,0:T(8,128)(2,1)} %bitcast.14, s32[1,32]{1,0:T(1,128)} %anchor_ref.3, s32[2,128]{1,0:T(2,128)} %bitcast.21), custom_call_target="tpu_custom_call" | custom-call | tf_op jit(solution)/shard_map/pallas_call | solution.py:67
  2.7 7.2 %all-to-all-start = ((bf16[8,32,768]{2,1,0:T(8,128)(2,1)}), bf16[8,32,768]{2,1,0:T(8,128)(2,1)S(1)}, u32[]{:S(2)}, u32[]{:S(2)}) async-start(bf16[8,32,768]{2,1,0:T(8,128)(2,1)} %get-tuple-element.41), calls=%async_computation | async-start | bytes 786432 | tf_op jit(solution)/shard_map/all_to_all | solution.py:502
  9.9 1.3 %collective-permute-start = (bf16[128,768]{1,0:T(8,128)(2,1)S(1)}, bf16[128,768]{1,0:T(8,128)(2,1)S(1)}, u32[]{:S(2)}, u32[]{:S(2)}) collective-permute-start(bf16[128,768]{1,0:T(8,128)(2,1)S(1)} %get-tuple-element.39), channel_id=1, source_target_pairs={{0,1},{1,2},{2,3},{3,4},{4,5},{5,6},{6,7},{7,8},{8,9},{9,10},{10,1... | collective-permute-start | bytes 589832 | tf_op jit(solution)/shard_map/ppermute | solution.py:428
  11.2 1.3 %collective-permute-start.1 = (bf16[128,768]{1,0:T(8,128)(2,1)S(1)}, bf16[128,768]{1,0:T(8,128)(2,1)S(1)}, u32[]{:S(2)}, u32[]{:S(2)}) collective-permute-start(bf16[128,768]{1,0:T(8,128)(2,1)S(1)} %get-tuple-element.40), channel_id=1, source_target_pairs={{1,0},{2,1},{3,2},{4,3},{5,4},{6,5},{7,6},{8,7},{9,8},{10,9},{11,1... | collective-permute-start | bytes 589832 | tf_op jit(solution)/shard_map/ppermute | solution.py:428
  12.5 4.0 %shard_map.122 = (bf16[256,768]{1,0:T(8,128)(2,1)S(1)}, bf16[256,768]{1,0:T(8,128)(2,1)S(1)}, bf16[256,768]{1,0:T(8,128)(2,1)S(1)}, bf16[256,768]{1,0:T(8,128)(2,1)S(1)}) custom-call(bf16[256,768]{1,0:T(8,128)(2,1)} %get-tuple-element.34.n_ref, bf16[256,768]{1,0:T(8,128)(2,1)} %bitcast.17, bf16[768,768]{1,0:T(8,128)(2,1)} %wq_any.1, ...), custom_call_target="tpu_custom_call" | custom-call | tf_op jit(solution)/shard_map/pallas_call | solution.py:88
  16.5 1.6 %all-to-all-done.an_ref = bf16[8,32,768]{2,1,0:T(8,128)(2,1)S(1)} async-done(((bf16[8,32,768]{2,1,0:T(8,128)(2,1)}), bf16[8,32,768]{2,1,0:T(8,128)(2,1)S(1)}, u32[]{:S(2)}, u32[]{:S(2)}) %all-to-all-start) | async-done | bytes 393248 | tf_op jit(solution)/shard_map/all_to_all | solution.py:502
  18.1 9.0 %shard_map.123 = (bf16[2048,768]{1,0:T(8,128)(2,1)S(1)}, bf16[512,768]{1,0:T(8,128)(2,1)}) custom-call(s32[2,3]{1,0:T(2,128)S(1)} %bitcast.10, s32[2]{0:T(128)S(1)} %bitcast.12, s32[1]{0:T(128)S(6)} %sub.3.side_ref, bf16[256,768]{1,0:T(8,128)(2,1)S(1)} %get-tuple-element.35.q_ref, bf16[256,768]{1,0:T(8,128)(2,1)S(1)} %get-tuple-element.36.k_ref, ...), custom_call_target="tpu_custom_call" | custom-call | tf_op jit(solution)/shard_map/pallas_call | solution.py:205
  27.1 1.6 %collective-permute-start.2 = (bf16[2048,768]{1,0:T(8,128)(2,1)S(1)}, bf16[2048,768]{1,0:T(8,128)(2,1)S(1)}, u32[]{:S(2)}, u32[]{:S(2)}) collective-permute-start(bf16[2048,768]{1,0:T(8,128)(2,1)S(1)} %get-tuple-element.42.first_ref.first_any), channel_id=1, source_target_pairs={{0,1},{1,0},{2,3},{3,2},{4,5},{5,4},{6,7},{7,6},{8,9},{9,8},{10,11... | collective-permute-start | bytes 9437192 | tf_op jit(solution)/shard_map/ppermute | solution.py:416
  28.8 6.6 %shard_map.124.own_ref.own_any = bf16[1024,768]{1,0:T(8,128)(2,1)S(1)} custom-call(s32[2,3]{1,0:T(2,128)S(1)} %bitcast.11, s32[2]{0:T(128)S(1)} %bitcast.13, s32[1]{0:T(128)} %bitcast.2.side_ref, bf16[256,768]{1,0:T(8,128)(2,1)S(1)} %get-tuple-element.35.q_ref, bf16[256,768]{1,0:T(8,128)(2,1)S(1)} %get-tuple-element.36.k_ref, ...), custom_call_target="tpu_custom_call" | custom-call | tf_op jit(solution)/shard_map/pallas_call | solution.py:217
  35.5 4.1 %shard_map.125 = bf16[32,96,384]{2,1,0:T(8,128)(2,1)} custom-call(bf16[2048,768]{1,0:T(8,128)(2,1)S(1)} %get-tuple-element.42.first_ref.first_any, bf16[1024,768]{1,0:T(8,128)(2,1)S(1)} %shard_map.124.own_ref.own_any, bf16[2048,768]{1,0:T(8,128)(2,1)S(1)} %collective-permute-done.2.got_ref), custom_call_target="tpu_custom_call" | custom-call | tf_op jit(solution)/shard_map/pallas_call | solution.py:264
  39.6 10.9 %all-to-all-start.1 = ((bf16[32,96,384]{2,1,0:T(8,128)(2,1)}), bf16[32,96,384]{2,1,0:T(8,128)(2,1)S(1)}, u32[]{:S(2)}, u32[]{:S(2)}) async-start(bf16[32,96,384]{2,1,0:T(8,128)(2,1)} %shard_map.125), calls=%async_computation.1 | async-start | bytes 4718592 | tf_op jit(solution)/shard_map/all_to_all | solution.py:514
  50.6 7.9 %shard_map.126 = (bf16[256,768]{1,0:T(8,128)(2,1)}, f32[256,768]{1,0:T(8,128)}, bf16[128,768]{1,0:T(8,128)(2,1)S(1)}, bf16[128,768]{1,0:T(8,128)(2,1)S(1)}, bf16...) custom-call(s32[3]{0:T(128)S(1)} %pad_add_fusion.place_ref, ...), custom_call_target="tpu_custom_call" | custom-call | tf_op jit(solution)/shard_map/pallas_call | solution.py:345
  58.5 1.3 %collective-permute-start.3 = (bf16[128,768]{1,0:T(8,128)(2,1)S(1)}, bf16[128,768]{1,0:T(8,128)(2,1)S(1)}, u32[]{:S(2)}, u32[]{:S(2)}) collective-permute-start(bf16[128,768]{1,0:T(8,128)(2,1)S(1)} %get-tuple-element.47), channel_id=1, source_target_pairs={{1,0},{2,1},{3,2},{4,3},{5,4},{6,5},{7,6},{8,7},{9,8},{10,9},{11,1... | collective-permute-start | bytes 589832 | tf_op jit(solution)/shard_map/ppermute | solution.py:428
  59.8 3.0 %collective-permute-start.4 = (bf16[128,768]{1,0:T(8,128)(2,1)S(1)}, bf16[128,768]{1,0:T(8,128)(2,1)S(1)}, u32[]{:S(2)}, u32[]{:S(2)}) collective-permute-start(bf16[128,768]{1,0:T(8,128)(2,1)S(1)} %get-tuple-element.50), channel_id=1, source_target_pairs={{0,1},{1,2},{2,3},{3,4},{4,5},{5,6},{6,7},{7,8},{8,9},{9,10},{10,1... | collective-permute-start | bytes 589832 | tf_op jit(solution)/shard_map/ppermute | solution.py:428
  63.2 2.7 %collective-permute-start.6 = (bf16[64,768]{1,0:T(8,128)(2,1)S(1)}, bf16[64,768]{1,0:T(8,128)(2,1)S(1)}, u32[]{:S(2)}, u32[]{:S(2)}) collective-permute-start(bf16[64,768]{1,0:T(8,128)(2,1)S(1)} %get-tuple-element.58), channel_id=1, source_target_pairs={{0,128},{64,192},{128,0},{192,64},{1,129},{65,193},{129,1},{193,65... | collective-permute-start | bytes 294920 | tf_op jit(solution)/shard_map/ppermute | solution.py:421
  65.9 17.4 %all-to-all-done.1.got_ref = bf16[32,96,384]{2,1,0:T(8,128)(2,1)S(1)} async-done(((bf16[32,96,384]{2,1,0:T(8,128)(2,1)}), bf16[32,96,384]{2,1,0:T(8,128)(2,1)S(1)}, u32[]{:S(2)}, u32[]{:S(2)}) %all-to-all-start.1) | async-done | bytes 2359328 | tf_op jit(solution)/shard_map/all_to_all | solution.py:514
  83.3 1.0 shard_map.127
  84.2 6.9 %all-to-all-start.2 = ((bf16[4,24,384]{2,1,0:T(8,128)(2,1)}), bf16[4,24,384]{2,1,0:T(8,128)(2,1)S(1)}, u32[]{:S(2)}, u32[]{:S(2)}) async-start(bf16[4,24,384]{2,1,0:T(8,128)(2,1)} %shard_map.127), calls=%async_computation.2 | async-start | bytes 147456 | tf_op jit(solution)/shard_map/all_to_all | solution.py:524
  91.2 1.2 %shard_map.128 = (f32[32,768]{1,0:T(8,128)}, bf16[32,768]{1,0:T(8,128)(2,1)S(1)}) custom-call(s32[3]{0:T(128)S(1)} %pad_add_fusion.place_ref, bf16[64,768]{1,0:T(8,128)(2,1)S(1)} %get-tuple-element.56.s0, bf16[64,768]{1,0:T(8,128)(2,1)S(1)} %collective-permute-done.5.s1, bf16[64,768]{1,0:T(8,128)(2,1)S(1)} %collective-permute-done.6.s2, ...), custom_call_target="tpu_custom_call" | custom-call | tf_op jit(solution)/shard_map/pallas_call | solution.py:371
  92.4 5.7 %collective-permute-start.8 = (bf16[32,768]{1,0:T(8,128)(2,1)S(1)}, bf16[32,768]{1,0:T(8,128)(2,1)S(1)}, u32[]{:S(2)}, u32[]{:S(2)}) collective-permute-start(bf16[32,768]{1,0:T(8,128)(2,1)S(1)} %get-tuple-element.61), channel_id=1, source_target_pairs={{0,32},{32,0},{1,33},{33,1},{2,34},{34,2},{3,35},{35,3},{4,36},{36... | collective-permute-start | bytes 147464 | tf_op jit(solution)/shard_map/ppermute | solution.py:416
  98.1 1.3 %all-to-all-done.2.rows_ref = bf16[4,24,384]{2,1,0:T(8,128)(2,1)S(1)} async-done(((bf16[4,24,384]{2,1,0:T(8,128)(2,1)}), bf16[4,24,384]{2,1,0:T(8,128)(2,1)S(1)}, u32[]{:S(2)}, u32[]{:S(2)}) %all-to-all-start.2) | async-done | bytes 73760 | tf_op jit(solution)/shard_map/all_to_all | solution.py:524
  100.0 0.7 collective-permute-start.9
  100.7 7.1 %collective-permute-start.10 = (f32[12,384]{1,0:T(8,128)S(1)}, f32[12,384]{1,0:T(8,128)S(1)}, u32[]{:S(2)}, u32[]{:S(2)}) collective-permute-start(f32[12,384]{1,0:T(8,128)S(1)} %get-tuple-element.64), channel_id=1, source_target_pairs={{192,193},{0,1},{64,65},{128,129},{193,225},{1,0},{65,64},{129,128... | collective-permute-start | bytes 55304 | tf_op jit(solution)/shard_map/ppermute | solution.py:470
  107.8 2.9 %shard_map.129 = bf16[256,768]{1,0:T(8,128)(2,1)} custom-call(bf16[256,768]{1,0:T(8,128)(2,1)} %bitcast.16, bf16[256,768]{1,0:T(8,128)(2,1)} %bitcast.19, f32[256,768]{1,0:T(8,128)} %get-tuple-element.53.own_ref, bf16[128,768]{1,0:T(8,128)(2,1)S(1)} %collective-permute-done.4.lo_ref, bf16[128,768]{1,0:T(8,128)(2,1)S(1)} %collective-permute-done.3.hi_ref, ...), custom_call_target="tpu_custom_call" | custom-call | tf_op jit(solution)/shard_map/pallas_call | solution.py:408
  (25 shorter events, 1.6 us)
Async XLA Ops:
  2.7 15.4 %all-to-all-start = ((bf16[8,32,768]{2,1,0:T(8,128)(2,1)}), bf16[8,32,768]{2,1,0:T(8,128)(2,1)S(1)}, u32[]{:S(2)}, u32[]{:S(2)}) async-start(bf16[8,32,768]{2,1,0:T(8,128)(2,1)} %get-tuple-element.41), calls=%async_computation | async-start | bytes 786432 | tf_op jit(solution)/shard_map/all_to_all | solution.py:502
  9.9 6.6 %collective-permute-start = (bf16[128,768]{1,0:T(8,128)(2,1)S(1)}, bf16[128,768]{1,0:T(8,128)(2,1)S(1)}, u32[]{:S(2)}, u32[]{:S(2)}) collective-permute-start(bf16[128,768]{1,0:T(8,128)(2,1)S(1)} %get-tuple-element.39), channel_id=1, source_target_pairs={{0,1},{1,2},{2,3},{3,4},{4,5},{5,6},{6,7},{7,8},{8,9},{9,10},{10,1... | collective-permute-start | bytes 589832 | tf_op jit(solution)/shard_map/ppermute | solution.py:428
  11.2 5.3 %collective-permute-start.1 = (bf16[128,768]{1,0:T(8,128)(2,1)S(1)}, bf16[128,768]{1,0:T(8,128)(2,1)S(1)}, u32[]{:S(2)}, u32[]{:S(2)}) collective-permute-start(bf16[128,768]{1,0:T(8,128)(2,1)S(1)} %get-tuple-element.40), channel_id=1, source_target_pairs={{1,0},{2,1},{3,2},{4,3},{5,4},{6,5},{7,6},{8,7},{9,8},{10,9},{11,1... | collective-permute-start | bytes 589832 | tf_op jit(solution)/shard_map/ppermute | solution.py:428
  12.5 5.6 %copy-start.2 = (s32[1,2,3]{2,1,0:T(2,128)S(1)}, s32[1,2,3]{2,1,0:T(2,128)}, u32[]{:S(2)}) copy-start(s32[1,2,3]{2,1,0:T(2,128)} %param.19) | copy-start | bytes 76
  12.5 5.6 %copy-start.3 = (s32[1,1,2]{2,1,0:T(1,128)S(1)}, s32[1,1,2]{2,1,0:T(1,128)}, u32[]{:S(2)}) copy-start(s32[1,1,2]{2,1,0:T(1,128)} %param.18) | copy-start | bytes 28
  27.1 8.3 %copy-start.1 = (bf16[2048,768]{1,0:T(8,128)(2,1)}, bf16[2048,768]{1,0:T(8,128)(2,1)S(1)}, u32[]{:S(2)}) copy-start(bf16[2048,768]{1,0:T(8,128)(2,1)S(1)} %get-tuple-element.42.first_ref.first_any) | copy-start | bytes 9437188
  27.1 8.3 %collective-permute-start.2 = (bf16[2048,768]{1,0:T(8,128)(2,1)S(1)}, bf16[2048,768]{1,0:T(8,128)(2,1)S(1)}, u32[]{:S(2)}, u32[]{:S(2)}) collective-permute-start(bf16[2048,768]{1,0:T(8,128)(2,1)S(1)} %get-tuple-element.42.first_ref.first_any), channel_id=1, source_target_pairs={{0,1},{1,0},{2,3},{3,2},{4,5},{5,4},{6,7},{7,6},{8,9},{9,8},{10,11... | collective-permute-start | bytes 9437192 | tf_op jit(solution)/shard_map/ppermute | solution.py:416
  35.4 4.2 %copy-start = (bf16[1024,768]{1,0:T(8,128)(2,1)}, bf16[1024,768]{1,0:T(8,128)(2,1)S(1)}, u32[]{:S(2)}) copy-start(bf16[1024,768]{1,0:T(8,128)(2,1)S(1)} %shard_map.124.own_ref.own_any) | copy-start | bytes 4718596
  39.6 43.7 %all-to-all-start.1 = ((bf16[32,96,384]{2,1,0:T(8,128)(2,1)}), bf16[32,96,384]{2,1,0:T(8,128)(2,1)S(1)}, u32[]{:S(2)}, u32[]{:S(2)}) async-start(bf16[32,96,384]{2,1,0:T(8,128)(2,1)} %shard_map.125), calls=%async_computation.1 | async-start | bytes 4718592 | tf_op jit(solution)/shard_map/all_to_all | solution.py:514
  58.5 7.4 %collective-permute-start.3 = (bf16[128,768]{1,0:T(8,128)(2,1)S(1)}, bf16[128,768]{1,0:T(8,128)(2,1)S(1)}, u32[]{:S(2)}, u32[]{:S(2)}) collective-permute-start(bf16[128,768]{1,0:T(8,128)(2,1)S(1)} %get-tuple-element.47), channel_id=1, source_target_pairs={{1,0},{2,1},{3,2},{4,3},{5,4},{6,5},{7,6},{8,7},{9,8},{10,9},{11,1... | collective-permute-start | bytes 589832 | tf_op jit(solution)/shard_map/ppermute | solution.py:428
  59.8 24.4 %collective-permute-start.4 = (bf16[128,768]{1,0:T(8,128)(2,1)S(1)}, bf16[128,768]{1,0:T(8,128)(2,1)S(1)}, u32[]{:S(2)}, u32[]{:S(2)}) collective-permute-start(bf16[128,768]{1,0:T(8,128)(2,1)S(1)} %get-tuple-element.50), channel_id=1, source_target_pairs={{0,1},{1,2},{2,3},{3,4},{4,5},{5,6},{6,7},{7,8},{8,9},{9,10},{10,1... | collective-permute-start | bytes 589832 | tf_op jit(solution)/shard_map/ppermute | solution.py:428
  62.9 28.3 %collective-permute-start.5 = (bf16[64,768]{1,0:T(8,128)(2,1)}, bf16[64,768]{1,0:T(8,128)(2,1)S(1)}, u32[]{:S(2)}, u32[]{:S(2)}) collective-permute-start(bf16[64,768]{1,0:T(8,128)(2,1)} %get-tuple-element.57), channel_id=1, source_target_pairs={{0,64},{64,128},{128,192},{192,0},{1,65},{65,129},{129,193},{193,1... | collective-permute-start | bytes 294920 | tf_op jit(solution)/shard_map/ppermute | solution.py:421
  63.2 28.0 %collective-permute-start.6 = (bf16[64,768]{1,0:T(8,128)(2,1)S(1)}, bf16[64,768]{1,0:T(8,128)(2,1)S(1)}, u32[]{:S(2)}, u32[]{:S(2)}) collective-permute-start(bf16[64,768]{1,0:T(8,128)(2,1)S(1)} %get-tuple-element.58), channel_id=1, source_target_pairs={{0,128},{64,192},{128,0},{192,64},{1,129},{65,193},{129,1},{193,65... | collective-permute-start | bytes 294920 | tf_op jit(solution)/shard_map/ppermute | solution.py:421
  65.9 25.3 %collective-permute-start.7 = (bf16[64,768]{1,0:T(8,128)(2,1)S(1)}, bf16[64,768]{1,0:T(8,128)(2,1)S(1)}, u32[]{:S(2)}, u32[]{:S(2)}) collective-permute-start(bf16[64,768]{1,0:T(8,128)(2,1)S(1)} %get-tuple-element.59), channel_id=1, source_target_pairs={{0,192},{64,0},{128,64},{192,128},{1,193},{65,1},{129,65},{193,129... | collective-permute-start | bytes 294920 | tf_op jit(solution)/shard_map/ppermute | solution.py:421
  84.2 15.2 %all-to-all-start.2 = ((bf16[4,24,384]{2,1,0:T(8,128)(2,1)}), bf16[4,24,384]{2,1,0:T(8,128)(2,1)S(1)}, u32[]{:S(2)}, u32[]{:S(2)}) async-start(bf16[4,24,384]{2,1,0:T(8,128)(2,1)} %shard_map.127), calls=%async_computation.2 | async-start | bytes 147456 | tf_op jit(solution)/shard_map/all_to_all | solution.py:524
  92.4 15.4 %collective-permute-start.8 = (bf16[32,768]{1,0:T(8,128)(2,1)S(1)}, bf16[32,768]{1,0:T(8,128)(2,1)S(1)}, u32[]{:S(2)}, u32[]{:S(2)}) collective-permute-start(bf16[32,768]{1,0:T(8,128)(2,1)S(1)} %get-tuple-element.61), channel_id=1, source_target_pairs={{0,32},{32,0},{1,33},{33,1},{2,34},{34,2},{3,35},{35,3},{4,36},{36... | collective-permute-start | bytes 147464 | tf_op jit(solution)/shard_map/ppermute | solution.py:416
  100.0 10.7 %collective-permute-start.9 = (f32[12,384]{1,0:T(8,128)S(1)}, f32[12,384]{1,0:T(8,128)S(1)}, u32[]{:S(2)}, u32[]{:S(2)}) collective-permute-start(f32[12,384]{1,0:T(8,128)S(1)} %get-tuple-element.63), channel_id=1, source_target_pairs={{192,192},{193,224},{224,193},{225,225},{194,194},{195,226},{226,1... | collective-permute-start | bytes 55304 | tf_op jit(solution)/shard_map/ppermute | solution.py:468
  100.7 10.0 %collective-permute-start.10 = (f32[12,384]{1,0:T(8,128)S(1)}, f32[12,384]{1,0:T(8,128)S(1)}, u32[]{:S(2)}, u32[]{:S(2)}) collective-permute-start(f32[12,384]{1,0:T(8,128)S(1)} %get-tuple-element.64), channel_id=1, source_target_pairs={{192,193},{0,1},{64,65},{128,129},{193,225},{1,0},{65,64},{129,128... | collective-permute-start | bytes 55304 | tf_op jit(solution)/shard_map/ppermute | solution.py:470
